TPU v7x, 32 devices: a whole 2x2x4 slice. The times are simulated.
32 devices in a mesh: rows: 4 (over z), seq: 8 (over y, x, core).
Axes of the slice: x: 2, y: 2, z: 4, core: 2. Of those that a mesh axis runs over, the one named last changes fastest.
Arguments:
- queries: bfloat16 [2048, 4096], P('seq'), may hold values from -50 to 50
- keys: bfloat16 [2048, 4096], P('seq'), may hold values from -6 to 6
- values: bfloat16 [2048, 4096], P('seq'), may hold values from -6 to 6
- grad_out: bfloat16 [4, 2048, 4096], P('rows', 'seq'), may hold values from -6 to 6
- table: bfloat16 [33, 4096], replicated, may hold values from -6 to 6
- positions: int32 [4], P('rows'), may hold values from 0 to 2047
- residues: int32 [4], P('rows'), may hold values from 4 to 23
- tiles: int32 [16, 8], replicated, may hold values from 0 to 15, as said below
- counts: int32 [16], replicated, may hold values from 1 to 8, as said below
Outputs:
- grad_queries: bfloat16 [4, 2048, 4096], P('rows', 'seq')
- grad_keys: bfloat16 [4, 2048, 4096], P('rows', 'seq')
- grad_values: bfloat16 [4, 2048, 4096], P('rows', 'seq')
Inputs may be any that keep to these rules, and one draw needn't show every extreme that they name: `tiles`: row i lists key blocks: entry 0 is i itself, the others differ from i and from each other. Only the first counts[i] entries of row i of tiles are used; some query block uses all 8.
All inputs are finite; a program needn't handle non-finite values.
Results may differ from a plain program's by a relative error of at most 0.0085.
Values may be sent and summed in bfloat16 or wider, within the bound.
A program may use at most 128 MiB of HBM per device.

v0:
```python
import math

import jax
import jax.numpy as jnp
from jax import lax
from jax.sharding import PartitionSpec as P

D_HEAD = 128
BLOCK = 128
TILES = 8


def substitute(grad_out, table, positions, residues, first_token):
    tok_count = grad_out.shape[1]
    spots = (
        jnp.arange(tok_count, dtype=jnp.int32)[None, :] + first_token == positions[:, None]
    ).astype(jnp.float32)
    picks = (jnp.arange(table.shape[0], dtype=jnp.int32)[None, :] == residues[:, None]).astype(
        jnp.bfloat16
    )
    added = jnp.dot(picks, table, preferred_element_type=jnp.float32)
    summed = grad_out.astype(jnp.float32) + spots[:, :, None] * added[:, None, :]
    return summed.astype(jnp.bfloat16)


def log_total(scores):
    row_max = jnp.max(scores, axis=(-2, -1), keepdims=True)
    return row_max + jnp.log(jnp.sum(jnp.exp(scores - row_max), axis=(-2, -1), keepdims=True))


def slot_mask(count_group):
    slots = jnp.arange(TILES, dtype=jnp.int32)
    return (slots[None, :] < count_group[:, None])[:, None, None, :, None]


def tile_onehot(tile_group, block_count):
    return (
        tile_group[:, :, None] == jnp.arange(block_count, dtype=jnp.int32)[None, None, :]
    ).astype(jnp.bfloat16)


def pick_tiles(blocks, onehot):
    return jnp.einsum("gtb,bkhd->gtkhd", onehot, blocks, preferred_element_type=jnp.float32).astype(
        jnp.bfloat16
    )


def add_tiles(total, terms, onehot):
    high_part = terms.astype(jnp.bfloat16)
    low_part = (terms - high_part.astype(jnp.float32)).astype(jnp.bfloat16)
    total = total + jnp.einsum(
        "gtb,rgtkhd->rbkhd", onehot, high_part, preferred_element_type=jnp.float32
    )
    return total + jnp.einsum(
        "gtb,rgtkhd->rbkhd", onehot, low_part, preferred_element_type=jnp.float32
    )


def tile_scores(query_group, key_blocks, onehot, live_slots, softmax_scale):
    key_tiles = pick_tiles(key_blocks, onehot)
    scores = (
        jnp.einsum("gqhd,gtkhd->ghqtk", query_group, key_tiles, preferred_element_type=jnp.float32)
        * softmax_scale
    )
    return (jnp.where(live_slots, scores, -1e30), key_tiles)


def block_stats(query_blocks, key_blocks, tiles, counts, first_block, block_total, softmax_scale):
    group = math.gcd(max(1, 512 // BLOCK), block_total)
    block_count = key_blocks.shape[0]

    def group_stats(group_index):
        offset_at = first_block + group_index * group
        query_group = lax.dynamic_slice_in_dim(query_blocks, offset_at, group, 0)
        tile_group = lax.dynamic_slice_in_dim(tiles, offset_at, group, 0)
        count_group = lax.dynamic_slice_in_dim(counts, offset_at, group, 0)
        scores, unused = tile_scores(
            query_group,
            key_blocks,
            tile_onehot(tile_group, block_count),
            slot_mask(count_group),
            softmax_scale,
        )
        return log_total(scores)[..., 0, 0]

    stacked = lax.map(group_stats, jnp.arange(block_total // group, dtype=jnp.int32))
    return stacked.reshape((block_total,) + stacked.shape[2:])


def per_device(queries, keys, values, grad_out, table, positions, residues, tiles, counts):
    tok_count = queries.shape[0]
    row_devices = lax.axis_size("rows")
    softmax_scale = D_HEAD ** (-0.5)
    query_heads, key_heads, value_heads = (
        lax.all_to_all(queries, "seq", split_axis=1, concat_axis=0, tiled=True),
        lax.all_to_all(keys, "seq", split_axis=1, concat_axis=0, tiled=True),
        lax.all_to_all(values, "seq", split_axis=1, concat_axis=0, tiled=True),
    )
    cotangent = substitute(grad_out, table, positions, residues, lax.axis_index("seq") * tok_count)
    cot_heads = lax.all_to_all(cotangent, "seq", split_axis=2, concat_axis=1, tiled=True)
    seq_len = query_heads.shape[0]
    width_local = query_heads.shape[1]
    heads_local = width_local // D_HEAD
    block_count = seq_len // BLOCK
    row_count = cot_heads.shape[0]
    block_shape = (block_count, BLOCK, heads_local, D_HEAD)
    query_blocks = query_heads.reshape(block_shape)
    key_blocks = key_heads.reshape(block_shape)
    value_blocks = value_heads.reshape(block_shape)
    cot_blocks = cot_heads.reshape((row_count,) + block_shape)
    share_count = block_count // row_devices
    own_stats = block_stats(
        query_blocks,
        key_blocks,
        tiles,
        counts,
        lax.axis_index("rows") * share_count,
        share_count,
        softmax_scale,
    )
    log_totals = lax.all_gather(own_stats, "rows", axis=0, tiled=True)
    group = math.gcd(max(1, 512 // BLOCK), block_count)

    def step(totals, group_index):
        grad_query, grad_keys, grad_values = totals
        offset_at = group_index * group
        query_group = lax.dynamic_slice_in_dim(query_blocks, offset_at, group, 0)
        tile_group = lax.dynamic_slice_in_dim(tiles, offset_at, group, 0)
        count_group = lax.dynamic_slice_in_dim(counts, offset_at, group, 0)
        stats_group = lax.dynamic_slice_in_dim(log_totals, offset_at, group, 0)
        cot_group = lax.dynamic_slice_in_dim(cot_blocks, offset_at, group, 1)
        live_slots = slot_mask(count_group)
        onehot = tile_onehot(tile_group, block_count)
        scores, key_tiles = tile_scores(query_group, key_blocks, onehot, live_slots, softmax_scale)
        value_tiles = pick_tiles(value_blocks, onehot)
        probs = jnp.where(live_slots, jnp.exp(scores - stats_group[:, :, :, None, None]), 0.0)
        probs_bf = probs.astype(jnp.bfloat16)
        grad_probs = jnp.einsum(
            "rgqhd,gtkhd->rghqtk", cot_group, value_tiles, preferred_element_type=jnp.float32
        )
        delta = jnp.sum(probs[None] * grad_probs, axis=(4, 5), keepdims=True)
        grad_scores = (probs[None] * (grad_probs - delta)).astype(jnp.bfloat16)
        query_terms = (
            softmax_scale
            * jnp.einsum(
                "rghqtk,gtkhd->rgqhd", grad_scores, key_tiles, preferred_element_type=jnp.float32
            )
        ).astype(jnp.bfloat16)
        key_terms = softmax_scale * jnp.einsum(
            "rghqtk,gqhd->rgtkhd", grad_scores, query_group, preferred_element_type=jnp.float32
        )
        value_terms = jnp.einsum(
            "ghqtk,rgqhd->rgtkhd", probs_bf, cot_group, preferred_element_type=jnp.float32
        )
        grad_keys = add_tiles(grad_keys, key_terms, onehot)
        grad_values = add_tiles(grad_values, value_terms, onehot)
        grad_query = lax.dynamic_update_slice_in_dim(grad_query, query_terms, offset_at, 1)
        return ((grad_query, grad_keys, grad_values), None)

    zeros_full = jnp.zeros((row_count,) + block_shape, jnp.float32)
    initial = (jnp.zeros((row_count,) + block_shape, jnp.bfloat16), zeros_full, zeros_full)
    finals, unused = lax.scan(step, initial, jnp.arange(block_count // group, dtype=jnp.int32))
    grad_query, grad_keys, grad_values = finals
    flat_shape = (row_count, seq_len, width_local)
    return (
        lax.all_to_all(
            grad_query.reshape(flat_shape), "seq", split_axis=1, concat_axis=2, tiled=True
        ),
        lax.all_to_all(
            grad_keys.reshape(flat_shape).astype(jnp.bfloat16),
            "seq",
            split_axis=1,
            concat_axis=2,
            tiled=True,
        ),
        lax.all_to_all(
            grad_values.reshape(flat_shape).astype(jnp.bfloat16),
            "seq",
            split_axis=1,
            concat_axis=2,
            tiled=True,
        ),
    )


def solution(mesh):
    placed = (
        P("seq", None),
        P("seq", None),
        P("seq", None),
        P("rows", "seq", None),
        P(),
        P("rows"),
        P("rows"),
        P(),
        P(),
    )
    return jax.shard_map(
        per_device,
        mesh=mesh,
        in_specs=placed,
        out_specs=(P("rows", "seq", None), P("rows", "seq", None), P("rows", "seq", None)),
        check_vma=False,
    )
```

profile of v0, /device:TPU:0, one launch (start us, length us, event | category | flops | bytes accessed | tf_op | source)
XLA Modules:
  0.0 689.8 jit_solution(5304286326911035727)
XLA Ops:
  4.5 7.3 %copy.236 = bf16[1,256,4096]{1,0,2:T(2,128)(2,1)} copy(bf16[1,256,4096]{2,1,0:T(8,128)(2,1)S(1)} %add_convert_fusion) | data formatting | bytes 4194304 | tf_op jit(solution)/shard_map/convert_element_type | solution.py:23
  12.3 21.6 %reduce.1 = bf16[4096,256]{1,0:T(8,128)(2,1)S(1)} reduce(bf16[4096,1,256]{2,1,0:T(2,128)(2,1)} %bitcast.293, bf16[]{:T(256)} %broadcast.138), dimensions={1}, to_apply=%bitcast.189.reduce_sub_computation | reduce | bytes 4194306
  46.3 22.6 %all-to-all-done.3 = bf16[8,2,65536]{2,1,0:T(2,128)(2,1)S(1)} async-done(((bf16[8,2,65536]{2,1,0:T(2,128)(2,1)}), bf16[8,2,65536]{2,1,0:T(2,128)(2,1)S(1)}, u32[]{:S(2)}, u32[]{:S(2)}) %all-to-all-start.3) | async-done | bytes 2097184 | tf_op jit(solution)/shard_map/all_to_all | solution.py:100
  77.3 22.6 %all-to-all-done.1 = bf16[256,8,512]{0,2,1:T(8,128)(2,1)} async-done(((bf16[256,8,512]{0,2,1:T(8,128)(2,1)}), bf16[256,8,512]{0,2,1:T(8,128)(2,1)}, u32[]{:S(2)}, u32[]{:S(2)}) %all-to-all-start.1) | async-done | bytes 2097184 | tf_op jit(solution)/shard_map/all_to_all | solution.py:95
  108.3 22.6 %all-to-all-done = bf16[256,8,512]{0,2,1:T(8,128)(2,1)} async-done(((bf16[256,8,512]{0,2,1:T(8,128)(2,1)}), bf16[256,8,512]{0,2,1:T(8,128)(2,1)}, u32[]{:S(2)}, u32[]{:S(2)}) %all-to-all-start) | async-done | bytes 2097184 | tf_op jit(solution)/shard_map/all_to_all | solution.py:96
  185.6 13.4 %all_gather.3 = f32[16,4,128]{2,1,0:T(4,128)S(1)} all-gather(f32[4,4,128]{2,1,0:T(4,128)S(1)} %bitcast.313), channel_id=1, replica_groups=mesh['rows'=4,'seq'=8] {'rows'}, dimensions={0}, use_global_device_ids=true | all-gather | bytes 40960 | tf_op jit(solution)/shard_map/all_gather | solution.py:121
  201.1 328.5 %while.5 = (s32[]{:T(128)}, bf16[1,16,128,4,128]{4,3,2,1,0:T(4,128)(2,1)}, f32[1,16,128,4,128]{4,1,3,2,0:T(8,128)}, f32[1,16,128,4,128]{4,1,3,2,0:T(8,128)}, s32...) while((s32[]{:T(128)}, ...), condition=%wide.region_4.5_spmd.clone, body=%wide.region_2.0_spmd.clone.sunk | while | flops 3160933376 | bytes 306767488 | solution.py:162
  238.8 6.8 bitcast_add_fusion.6
  251.7 7.9 %copy.334 = bf16[4,8,128,4,128]{4,1,0,3,2:T(8,128)(2,1)} copy(bf16[4,8,128,4,128]{2,4,1,3,0:T(8,128)(2,1)} %fusion.152) | data formatting | bytes 8388608 | tf_op jit(solution)/shard_map/reshape.24
  264.6 7.9 %copy.335 = bf16[4,8,128,4,128]{4,1,0,3,2:T(8,128)(2,1)} copy(bf16[4,8,128,4,128]{2,4,1,3,0:T(8,128)(2,1)} %fusion.154) | data formatting | bytes 8388608 | tf_op jit(solution)/shard_map/reshape.26
  272.4 6.4 bitcast_add_fusion.7
  316.3 9.1 %bitcast_add_fusion.6 = f32[1,16,128,4,128]{4,1,3,2,0:T(8,128)} fusion(f32[128,4,128,16,1]{2,3,4,1,0:T(8,128)S(1)} %fusion.149, f32[1,16,128,4,128]{4,1,3,2,0:T(8,128)} %get-tuple-element.352, bf16[4,8,128,4,128]{4,2,1,3,0:T(8,128)(2,1)S(1)} %fusion.150, pred[]{:T(512)S(6)} %compare.3, s32[4,8]{1,0:T(4,128)S(1)} %constant_dynamic-slice_fusion.8), kind=kOutput, calls=%fused_computation.18.clone.1 | convolution fusion | flops 70255104 | bytes 16777344 | tf_op jit(solution)/shard_map/while/body/eval_jaxpr/gtb,rgtkhd->rbkhd/dot_general | solution.py:51
  331.5 7.9 %copy.334 = bf16[4,8,128,4,128]{4,1,0,3,2:T(8,128)(2,1)} copy(bf16[4,8,128,4,128]{2,4,1,3,0:T(8,128)(2,1)} %fusion.152) | data formatting | bytes 8388608 | tf_op jit(solution)/shard_map/reshape.24
  344.4 7.9 %copy.335 = bf16[4,8,128,4,128]{4,1,0,3,2:T(8,128)(2,1)} copy(bf16[4,8,128,4,128]{2,4,1,3,0:T(8,128)(2,1)} %fusion.154) | data formatting | bytes 8388608 | tf_op jit(solution)/shard_map/reshape.26
  352.2 7.5 %bitcast_add_fusion.7 = f32[1,16,128,4,128]{4,1,3,2,0:T(8,128)} fusion(f32[128,4,128,16,1]{2,3,4,1,0:T(8,128)} %fusion.153, f32[1,16,128,4,128]{4,1,3,2,0:T(8,128)} %get-tuple-element.353, bf16[4,8,128,4,128]{4,1,0,3,2:T(8,128)(2,1)} %copy.335, pred[]{:T(512)S(6)} %compare.3, s32[4,8]{1,0:T(4,128)S(1)} %constant_dynamic-slice_fusion.8), kind=kOutput, calls=%fused_computation.16.clone.1 | convolution fusion | flops 70255104 | bytes 16777344 | tf_op jit(solution)/shard_map/while/body/eval_jaxpr/gtb,rgtkhd->rbkhd/dot_general | solution.py:54
  397.3 9.1 %bitcast_add_fusion.6 = f32[1,16,128,4,128]{4,1,3,2,0:T(8,128)} fusion(f32[128,4,128,16,1]{2,3,4,1,0:T(8,128)S(1)} %fusion.149, f32[1,16,128,4,128]{4,1,3,2,0:T(8,128)} %get-tuple-element.352, bf16[4,8,128,4,128]{4,2,1,3,0:T(8,128)(2,1)S(1)} %fusion.150, pred[]{:T(512)S(6)} %compare.3, s32[4,8]{1,0:T(4,128)S(1)} %constant_dynamic-slice_fusion.8), kind=kOutput, calls=%fused_computation.18.clone.1 | convolution fusion | flops 70255104 | bytes 16777344 | tf_op jit(solution)/shard_map/while/body/eval_jaxpr/gtb,rgtkhd->rbkhd/dot_general | solution.py:51
  412.5 7.9 %copy.334 = bf16[4,8,128,4,128]{4,1,0,3,2:T(8,128)(2,1)} copy(bf16[4,8,128,4,128]{2,4,1,3,0:T(8,128)(2,1)} %fusion.152) | data formatting | bytes 8388608 | tf_op jit(solution)/shard_map/reshape.24
  425.3 7.9 %copy.335 = bf16[4,8,128,4,128]{4,1,0,3,2:T(8,128)(2,1)} copy(bf16[4,8,128,4,128]{2,4,1,3,0:T(8,128)(2,1)} %fusion.154) | data formatting | bytes 8388608 | tf_op jit(solution)/shard_map/reshape.26
  433.2 7.5 %bitcast_add_fusion.7 = f32[1,16,128,4,128]{4,1,3,2,0:T(8,128)} fusion(f32[128,4,128,16,1]{2,3,4,1,0:T(8,128)} %fusion.153, f32[1,16,128,4,128]{4,1,3,2,0:T(8,128)} %get-tuple-element.353, bf16[4,8,128,4,128]{4,1,0,3,2:T(8,128)(2,1)} %copy.335, pred[]{:T(512)S(6)} %compare.3, s32[4,8]{1,0:T(4,128)S(1)} %constant_dynamic-slice_fusion.8), kind=kOutput, calls=%fused_computation.16.clone.1 | convolution fusion | flops 70255104 | bytes 16777344 | tf_op jit(solution)/shard_map/while/body/eval_jaxpr/gtb,rgtkhd->rbkhd/dot_general | solution.py:54
  478.3 9.1 %bitcast_add_fusion.6 = f32[1,16,128,4,128]{4,1,3,2,0:T(8,128)} fusion(f32[128,4,128,16,1]{2,3,4,1,0:T(8,128)S(1)} %fusion.149, f32[1,16,128,4,128]{4,1,3,2,0:T(8,128)} %get-tuple-element.352, bf16[4,8,128,4,128]{4,2,1,3,0:T(8,128)(2,1)S(1)} %fusion.150, pred[]{:T(512)S(6)} %compare.3, s32[4,8]{1,0:T(4,128)S(1)} %constant_dynamic-slice_fusion.8), kind=kOutput, calls=%fused_computation.18.clone.1 | convolution fusion | flops 70255104 | bytes 16777344 | tf_op jit(solution)/shard_map/while/body/eval_jaxpr/gtb,rgtkhd->rbkhd/dot_general | solution.py:51
  493.5 7.9 %copy.334 = bf16[4,8,128,4,128]{4,1,0,3,2:T(8,128)(2,1)} copy(bf16[4,8,128,4,128]{2,4,1,3,0:T(8,128)(2,1)} %fusion.152) | data formatting | bytes 8388608 | tf_op jit(solution)/shard_map/reshape.24
  506.3 7.9 %copy.335 = bf16[4,8,128,4,128]{4,1,0,3,2:T(8,128)(2,1)} copy(bf16[4,8,128,4,128]{2,4,1,3,0:T(8,128)(2,1)} %fusion.154) | data formatting | bytes 8388608 | tf_op jit(solution)/shard_map/reshape.26
  514.2 7.5 %bitcast_add_fusion.7 = f32[1,16,128,4,128]{4,1,3,2,0:T(8,128)} fusion(f32[128,4,128,16,1]{2,3,4,1,0:T(8,128)} %fusion.153, f32[1,16,128,4,128]{4,1,3,2,0:T(8,128)} %get-tuple-element.353, bf16[4,8,128,4,128]{4,1,0,3,2:T(8,128)(2,1)} %copy.335, pred[]{:T(512)S(6)} %compare.3, s32[4,8]{1,0:T(4,128)S(1)} %constant_dynamic-slice_fusion.8), kind=kOutput, calls=%fused_computation.16.clone.1 | convolution fusion | flops 70255104 | bytes 16777344 | tf_op jit(solution)/shard_map/while/body/eval_jaxpr/gtb,rgtkhd->rbkhd/dot_general | solution.py:54
  539.5 14.1 %reduce.4 = bf16[2048,512]{1,0:T(8,128)(2,1)S(1)} reduce(bf16[2048,1,512]{2,1,0:T(2,128)(2,1)} %bitcast.296, bf16[]{:T(256)} %broadcast.138), dimensions={1}, to_apply=%bitcast.195.reduce_sub_computation | reduce | bytes 4194306
  566.5 12.6 %reshape.255 = bf16[1,2048,512]{2,0,1:T(2,128)(2,1)} reshape(bf16[1,16,128,4,128]{4,3,2,1,0:T(4,128)(2,1)} %copy.270) | data formatting | bytes 4194304 | tf_op jit(solution)/shard_map/convert_element_type | solution.py:170
  579.1 15.4 %reduce.3 = bf16[2048,512]{1,0:T(8,128)(2,1)} reduce(bf16[2048,1,512]{2,1,0:T(2,128)(2,1)} %bitcast.297, bf16[]{:T(256)} %broadcast.138), dimensions={1}, to_apply=%bitcast.193.reduce_sub_computation | reduce | bytes 4194306
  594.5 6.3 reshape.261
  605.1 12.6 %reshape.254 = bf16[1,2048,512]{2,0,1:T(2,128)(2,1)} reshape(bf16[1,16,128,4,128]{4,3,2,1,0:T(4,128)(2,1)} %get-tuple-element.88) | data formatting | bytes 4194304 | tf_op jit(solution)/shard_map/reshape | solution.py:167
  617.7 15.4 %reduce.2 = bf16[2048,512]{1,0:T(8,128)(2,1)} reduce(bf16[2048,1,512]{2,1,0:T(2,128)(2,1)} %bitcast.294, bf16[]{:T(256)} %broadcast.138), dimensions={1}, to_apply=%bitcast.191.reduce_sub_computation | reduce | bytes 4194306
  633.1 6.3 reshape.259
  657.6 6.7 reshape.262
  673.6 6.7 reshape.260
  (226 shorter events, 343.8 us)
Async XLA Ops:
  37.1 31.8 %all-to-all-start.3 = ((bf16[8,2,65536]{2,1,0:T(2,128)(2,1)}), bf16[8,2,65536]{2,1,0:T(2,128)(2,1)S(1)}, u32[]{:S(2)}, u32[]{:S(2)}) async-start(bf16[8,2,65536]{2,1,0:T(2,128)(2,1)} %reshape.257), calls=%async_computation.3 | async-start | bytes 4194304 | tf_op jit(solution)/shard_map/all_to_all | solution.py:100
  68.9 31.0 %all-to-all-start.1 = ((bf16[256,8,512]{0,2,1:T(8,128)(2,1)}), bf16[256,8,512]{0,2,1:T(8,128)(2,1)}, u32[]{:S(2)}, u32[]{:S(2)}) async-start(bf16[256,8,512]{0,2,1:T(8,128)(2,1)} %bitcast.306), calls=%async_computation.1 | async-start | bytes 4194304 | tf_op jit(solution)/shard_map/all_to_all | solution.py:95
  99.9 31.0 %all-to-all-start = ((bf16[256,8,512]{0,2,1:T(8,128)(2,1)}), bf16[256,8,512]{0,2,1:T(8,128)(2,1)}, u32[]{:S(2)}, u32[]{:S(2)}) async-start(bf16[256,8,512]{0,2,1:T(8,128)(2,1)} %bitcast.307), calls=%async_computation | async-start | bytes 4194304 | tf_op jit(solution)/shard_map/all_to_all | solution.py:96
  104.2 31.4 %copy-start.7 = (s32[16,8]{0,1:T(8,128)S(1)}, s32[16,8]{0,1:T(8,128)}, u32[]{:S(2)}) copy-start(s32[16,8]{0,1:T(8,128)} %param.18) | copy-start | bytes 1540
  104.3 31.4 %copy-start.8 = (s32[16]{0:T(128)S(1)}, s32[16]{0:T(128)}, u32[]{:S(2)}) copy-start(s32[16]{0:T(128)} %param.19) | copy-start | bytes 196
  130.9 33.7 %all-to-all-start.2 = ((bf16[256,8,512]{0,2,1:T(8,128)(2,1)}), bf16[256,8,512]{0,2,1:T(8,128)(2,1)}, u32[]{:S(2)}, u32[]{:S(2)}) async-start(bf16[256,8,512]{0,2,1:T(8,128)(2,1)} %bitcast.305), calls=%async_computation.2 | async-start | bytes 4194304 | tf_op jit(solution)/shard_map/all_to_all | solution.py:97
  201.3 5.4 copy-start.3
  234.7 10.9 %slice-start = ((s8[8388608]{0:T(1024)(128)(4,1)}), s8[4194304]{0:T(1024)(128)(4,1)S(1)}, s32[]{:S(2)}) async-start(s8[8388608]{0:T(1024)(128)(4,1)} %bitcast.288), calls=%async_computation.7 | async-start | bytes 8388608 | tf_op jit(solution)/shard_map/while
  238.8 6.8 slice-start.1
  272.4 6.4 copy-start.4
  278.8 5.4 copy-start.3
  297.2 3.0 copy-start.2
  297.2 3.0 copy-start.5
  312.2 13.3 %slice-start = ((s8[8388608]{0:T(1024)(128)(4,1)}), s8[4194304]{0:T(1024)(128)(4,1)S(1)}, s32[]{:S(2)}) async-start(s8[8388608]{0:T(1024)(128)(4,1)} %bitcast.288), calls=%async_computation.7 | async-start | bytes 8388608 | tf_op jit(solution)/shard_map/while
  316.3 9.2 %slice-start.1 = ((s8[8388608]{0:T(1024)(128)(4,1)}), s8[4194304]{0:T(1024)(128)(4,1)S(1)}, s32[]{:S(2)}) async-start(s8[8388608]{0:T(1024)(128)(4,1)} %bitcast.288), calls=%async_computation.8 | async-start | bytes 8388608 | tf_op jit(solution)/shard_map/while
  352.2 7.6 %copy-start.4 = (bf16[16,128,4,128]{3,0,2,1:T(8,128)(2,1)S(1)}, bf16[16,128,4,128]{3,0,2,1:T(8,128)(2,1)}, u32[]{:S(2)}) copy-start(bf16[16,128,4,128]{3,0,2,1:T(8,128)(2,1)} %copy-done.3) | copy-start | bytes 6291460 | tf_op jit(solution)/shard_map/while
  359.8 5.4 copy-start.3
  378.2 3.0 copy-start.2
  378.2 3.0 copy-start.5
  393.1 13.3 %slice-start = ((s8[8388608]{0:T(1024)(128)(4,1)}), s8[4194304]{0:T(1024)(128)(4,1)S(1)}, s32[]{:S(2)}) async-start(s8[8388608]{0:T(1024)(128)(4,1)} %bitcast.288), calls=%async_computation.7 | async-start | bytes 8388608 | tf_op jit(solution)/shard_map/while
  397.3 9.2 %slice-start.1 = ((s8[8388608]{0:T(1024)(128)(4,1)}), s8[4194304]{0:T(1024)(128)(4,1)S(1)}, s32[]{:S(2)}) async-start(s8[8388608]{0:T(1024)(128)(4,1)} %bitcast.288), calls=%async_computation.8 | async-start | bytes 8388608 | tf_op jit(solution)/shard_map/while
  433.2 7.6 %copy-start.4 = (bf16[16,128,4,128]{3,0,2,1:T(8,128)(2,1)S(1)}, bf16[16,128,4,128]{3,0,2,1:T(8,128)(2,1)}, u32[]{:S(2)}) copy-start(bf16[16,128,4,128]{3,0,2,1:T(8,128)(2,1)} %copy-done.3) | copy-start | bytes 6291460 | tf_op jit(solution)/shard_map/while
  440.8 5.4 copy-start.3
  459.1 3.0 copy-start.2
  459.2 3.0 copy-start.5
  474.1 13.3 %slice-start = ((s8[8388608]{0:T(1024)(128)(4,1)}), s8[4194304]{0:T(1024)(128)(4,1)S(1)}, s32[]{:S(2)}) async-start(s8[8388608]{0:T(1024)(128)(4,1)} %bitcast.288), calls=%async_computation.7 | async-start | bytes 8388608 | tf_op jit(solution)/shard_map/while
  478.3 9.2 %slice-start.1 = ((s8[8388608]{0:T(1024)(128)(4,1)}), s8[4194304]{0:T(1024)(128)(4,1)S(1)}, s32[]{:S(2)}) async-start(s8[8388608]{0:T(1024)(128)(4,1)} %bitcast.288), calls=%async_computation.8 | async-start | bytes 8388608 | tf_op jit(solution)/shard_map/while
  514.2 7.6 %copy-start.4 = (bf16[16,128,4,128]{3,0,2,1:T(8,128)(2,1)S(1)}, bf16[16,128,4,128]{3,0,2,1:T(8,128)(2,1)}, u32[]{:S(2)}) copy-start(bf16[16,128,4,128]{3,0,2,1:T(8,128)(2,1)} %copy-done.3) | copy-start | bytes 6291460 | tf_op jit(solution)/shard_map/while
  557.4 43.4 %all-to-all-start.6 = ((bf16[8,2,65536]{2,1,0:T(2,128)(2,1)}), bf16[8,2,65536]{2,1,0:T(2,128)(2,1)S(1)}, u32[]{:S(2)}, u32[]{:S(2)}) async-start(bf16[8,2,65536]{2,1,0:T(2,128)(2,1)} %reshape.263), calls=%async_computation.6 | async-start | bytes 4194304 | tf_op jit(solution)/shard_map/all_to_all | solution.py:176
  600.8 38.6 %all-to-all-start.5 = ((bf16[8,2,65536]{2,1,0:T(2,128)(2,1)}), bf16[8,2,65536]{2,1,0:T(2,128)(2,1)}, u32[]{:S(2)}, u32[]{:S(2)}) async-start(bf16[8,2,65536]{2,1,0:T(2,128)(2,1)} %reshape.261), calls=%async_computation.5 | async-start | bytes 4194304 | tf_op jit(solution)/shard_map/all_to_all | solution.py:169
  639.4 34.2 %all-to-all-start.4 = ((bf16[8,2,65536]{2,1,0:T(2,128)(2,1)}), bf16[8,2,65536]{2,1,0:T(2,128)(2,1)}, u32[]{:S(2)}, u32[]{:S(2)}) async-start(bf16[8,2,65536]{2,1,0:T(2,128)(2,1)} %reshape.259), calls=%async_computation.4 | async-start | bytes 4194304 | tf_op jit(solution)/shard_map/all_to_all | solution.py:166
  683.1 6.5 copy-start.1
  (7 other events, 17.2 us)
where the time goes:
time: 699 us; the launch traced here: 690 us
  local copies, waits for them, and re-layouts  255 us (36%)
  matrix products  186 us (27%)
  other arithmetic  122 us (17%)
  waiting for transfers between devices  67.7 us (10%)
  starting transfers between devices  31.6 us (5%)
  blocking collectives  13.4 us (2%)
  loops' own time  11.3 us (2%)
    unnamed x31, local copies, waits for them, and re-layouts  92 us
    unnamed x6, other arithmetic  66.3 us
    another operation x8, local copies, waits for them, and re-layouts  63.1 us
    dot_general x8, matrix products, add_tiles(): jnp.einsum('gtb,rgtkhd->rbkhd', onehot, high_part, preferred_element_type...  54.2 us
    another operation x20, other arithmetic  46 us
    dot_general x8, matrix products, add_tiles(): jnp.einsum('gtb,rgtkhd->rbkhd', onehot, low_part, preferred_element_type=...  45.4 us
    all_to_all x1, waiting for transfers between devices, per_device(): lax.all_to_all(queries, 'seq', split_axis=1, concat_axis=0, tiled=True)  22.6 us
    all_to_all x1, waiting for transfers between devices, per_device(): lax.all_to_all(cotangent, 'seq', split_axis=2, concat_axis=1, tiled=True)  22.6 us
  transfers between devices with their start and end apart: 7, of which 3 were waited for; matrix products, arithmetic and copies ran while one was open for 21% of the time, Pallas kernels for 0%

commit v1 on v0

v1 whole, which is shorter than its diff:
```python
import functools

import jax
import jax.numpy as jnp
from jax import lax
from jax.experimental import pallas as pl
from jax.experimental.pallas import tpu as pltpu
from jax.sharding import PartitionSpec as P

D_HEAD = 128
BLOCK = 128
CHUNKS = 2
NEG = -1e30
VMEM_LIMIT = 56 * 1024 * 1024


def pack_kernel(heads, spot_ref, q_ref, k_ref, v_ref, g_ref, table_ref, out_ref):
    for a, ref in enumerate((q_ref, k_ref, v_ref)):
        for h in range(heads):
            out_ref[0, a, h] = ref[:, h * D_HEAD : (h + 1) * D_HEAD]
    tok_count = q_ref.shape[0]
    here = spot_ref[0]
    added = table_ref[pl.ds(spot_ref[1], 1), :]
    rows = lax.broadcasted_iota(jnp.int32, (tok_count, 1), 0)
    for h in range(heads):
        cols = slice(h * D_HEAD, (h + 1) * D_HEAD)
        out_ref[0, 3, h] = g_ref[0, :, cols]

    @pl.when((here >= 0) & (here < tok_count))
    def substitute():
        for h in range(heads):
            cols = slice(h * D_HEAD, (h + 1) * D_HEAD)
            term = jnp.where(rows == here, added[:, cols], 0.0)
            out_ref[0, 3, h] = (g_ref[0, :, cols].astype(jnp.float32) + term).astype(jnp.bfloat16)


def pack(chunk, devices, heads, spot, queries, keys, values, grad_out, table):
    tok_count = queries.shape[0]
    width = heads * D_HEAD
    wide = pl.BlockSpec((tok_count, width), lambda d, s: (0, d * CHUNKS + chunk))
    return pl.pallas_call(
        functools.partial(pack_kernel, heads),
        grid_spec=pltpu.PrefetchScalarGridSpec(
            num_scalar_prefetch=1,
            grid=(devices,),
            in_specs=[
                wide,
                wide,
                wide,
                pl.BlockSpec((1, tok_count, width), lambda d, s: (0, 0, d * CHUNKS + chunk)),
                pl.BlockSpec((table.shape[0], width), lambda d, s: (0, d * CHUNKS + chunk)),
            ],
            out_specs=pl.BlockSpec(
                (1, 4, heads, tok_count, D_HEAD), lambda d, s: (d, 0, 0, 0, 0)
            ),
        ),
        out_shape=jax.ShapeDtypeStruct((devices, 4, heads, tok_count, D_HEAD), jnp.bfloat16),
        compiler_params=pltpu.CompilerParams(vmem_limit_bytes=VMEM_LIMIT),
        cost_estimate=pl.CostEstimate(
            flops=0, bytes_accessed=16 * devices * heads * tok_count * D_HEAD, transcendentals=0
        ),
        name="pack",
    )(spot, queries, keys, values, grad_out, table)


def attend_kernel(heads, block_total, slots, per, tiles_ref, counts_ref, x_ref, out_ref, kt_ref, dk_ref, dv_ref):
    scale = D_HEAD ** (-0.5)
    nt = (((1,), (1,)), ((), ()))
    nn = (((1,), (0,)), ((), ()))
    dk_ref[...] = jnp.zeros_like(dk_ref)
    dv_ref[...] = jnp.zeros_like(dv_ref)

    def rows_of(block):
        return block // per, pl.ds(pl.multiple_of((block % per) * BLOCK, BLOCK), BLOCK)

    def turn(block, carry):
        dev, rows = rows_of(block)
        for h in range(heads):
            kt_ref[h, block] = x_ref[dev, 1, h, rows, :].astype(jnp.float32).T.astype(jnp.bfloat16)
        return carry

    lax.fori_loop(0, block_total, turn, 0)

    def attend(block, used):
        count = counts_ref[block]
        dev, rows = rows_of(block)
        listed = [tiles_ref[block, j] for j in range(used)]
        places = [rows_of(t) for t in listed]
        for h in range(heads):
            q = x_ref[dev, 0, h, rows, :]
            cot = x_ref[dev, 3, h, rows, :]
            ks = jnp.concatenate([x_ref[d, 1, h, r, :] for d, r in places], axis=0)
            vs = jnp.concatenate([x_ref[d, 2, h, r, :] for d, r in places], axis=0)
            kts = jnp.concatenate([kt_ref[h, t] for t in listed], axis=1)
            scores = lax.dot_general(ks, q, nt, preferred_element_type=jnp.float32)
            if used > 1:
                last = jnp.where(count >= used, scores[(used - 1) * BLOCK :], NEG)
                scores = jnp.concatenate([scores[: (used - 1) * BLOCK], last], axis=0)
            row_max = jnp.max(scores, axis=0, keepdims=True)
            weights = jnp.exp((scores - row_max) * scale)
            probs = weights * (1.0 / jnp.sum(weights, axis=0, keepdims=True))
            grad_probs = lax.dot_general(vs, cot, nt, preferred_element_type=jnp.float32)
            delta = jnp.sum(probs * grad_probs, axis=0, keepdims=True)
            grad_scores = (probs * (grad_probs - delta)).astype(jnp.bfloat16)
            value_terms = lax.dot_general(
                probs.astype(jnp.bfloat16), cot, nn, preferred_element_type=jnp.float32
            )
            key_terms = lax.dot_general(grad_scores, q, nn, preferred_element_type=jnp.float32)
            query_t = lax.dot_general(kts, grad_scores, nn, preferred_element_type=jnp.float32)
            out_ref[dev, 0, h, rows, :] = (scale * query_t.T).astype(jnp.bfloat16)
            for j, t in enumerate(listed):
                part = slice(j * BLOCK, (j + 1) * BLOCK)
                dv_ref[h, t] += value_terms[part]
                dk_ref[h, t] += key_terms[part]

    sizes = list(range(2, slots + 1, 2))

    def step(block, carry):
        count = counts_ref[block]
        for used in sizes:

            @pl.when((count <= used) & (count > used - 2))
            def run(used=used):
                attend(block, used)

        return carry

    lax.fori_loop(0, block_total, step, 0)

    def close(block, carry):
        dev, rows = rows_of(block)
        for h in range(heads):
            out_ref[dev, 1, h, rows, :] = (scale * dk_ref[h, block]).astype(jnp.bfloat16)
            out_ref[dev, 2, h, rows, :] = dv_ref[h, block].astype(jnp.bfloat16)
        return carry

    lax.fori_loop(0, block_total, close, 0)


def attend(tiles, counts, packed):
    devices, _, heads, tok_count, _ = packed.shape
    block_total, slots = tiles.shape
    per = tok_count // BLOCK
    vmem = pl.BlockSpec(memory_space=pltpu.VMEM)
    smem = pl.BlockSpec(memory_space=pltpu.SMEM)
    return pl.pallas_call(
        functools.partial(attend_kernel, heads, block_total, slots, per),
        in_specs=[smem, smem, vmem],
        out_specs=vmem,
        out_shape=jax.ShapeDtypeStruct((devices, 3, heads, tok_count, D_HEAD), jnp.bfloat16),
        scratch_shapes=[
            pltpu.VMEM((heads, block_total, D_HEAD, BLOCK), jnp.bfloat16),
            pltpu.VMEM((heads, block_total, BLOCK, D_HEAD), jnp.float32),
            pltpu.VMEM((heads, block_total, BLOCK, D_HEAD), jnp.float32),
        ],
        compiler_params=pltpu.CompilerParams(vmem_limit_bytes=VMEM_LIMIT),
        cost_estimate=pl.CostEstimate(
            flops=40 * heads * block_total * slots * BLOCK * BLOCK * D_HEAD,
            bytes_accessed=2 * 7 * heads * devices * tok_count * D_HEAD,
            transcendentals=heads * block_total * slots * BLOCK * BLOCK,
        ),
        name="attend",
    )(tiles, counts, packed)


def unpack_kernel(heads, *refs):
    ins, outs = refs[:CHUNKS], refs[CHUNKS:]
    for a, out in enumerate(outs):
        for c, ref in enumerate(ins):
            for h in range(heads):
                at = (c * heads + h) * D_HEAD
                out[0, :, at : at + D_HEAD] = ref[0, a, h]


def unpack(parts):
    devices, _, heads, tok_count, _ = parts[0].shape
    width = CHUNKS * heads * D_HEAD
    shape = jax.ShapeDtypeStruct((1, tok_count, devices * width), jnp.bfloat16)
    return pl.pallas_call(
        functools.partial(unpack_kernel, heads),
        grid=(devices,),
        in_specs=[pl.BlockSpec((1, 3, heads, tok_count, D_HEAD), lambda d: (d, 0, 0, 0, 0))] * CHUNKS,
        out_specs=[pl.BlockSpec((1, tok_count, width), lambda d: (0, 0, d))] * 3,
        out_shape=[shape] * 3,
        compiler_params=pltpu.CompilerParams(vmem_limit_bytes=VMEM_LIMIT),
        name="unpack",
    )(*parts)


def per_device(queries, keys, values, grad_out, table, positions, residues, tiles, counts):
    devices = lax.axis_size("seq")
    tok_count, width = queries.shape
    heads = width // D_HEAD // devices // CHUNKS
    spot = jnp.concatenate([positions - lax.axis_index("seq") * tok_count, residues])
    table32 = table.astype(jnp.float32)
    received = []
    for chunk in range(CHUNKS):
        packed = pack(chunk, devices, heads, spot, queries, keys, values, grad_out, table32)
        received.append(lax.all_to_all(packed, "seq", split_axis=0, concat_axis=0, tiled=True))
    parts = []
    for chunk in range(CHUNKS):
        grads = attend(tiles, counts, received[chunk])
        parts.append(lax.all_to_all(grads, "seq", split_axis=0, concat_axis=0, tiled=True))
    return tuple(unpack(parts))


def solution(mesh):
    placed = (
        P("seq", None),
        P("seq", None),
        P("seq", None),
        P("rows", "seq", None),
        P(),
        P("rows"),
        P("rows"),
        P(),
        P(),
    )
    return jax.shard_map(
        per_device,
        mesh=mesh,
        in_specs=placed,
        out_specs=(P("rows", "seq", None), P("rows", "seq", None), P("rows", "seq", None)),
        check_vma=False,
    )
```

time: 699 us -> 213 us (0.30); the launches traced: 690 us -> 212 us
  local copies, waits for them, and re-layouts: 255 us -> 0.68 us
  matrix products: 186 us -> 0 us
  other arithmetic: 122 us -> 2.44 us
  Pallas kernels: 0 us -> 79.6 us
  blocking collectives: 13.4 us -> 42.3 us
  starting transfers between devices: 31.6 us -> 13.2 us
  loops' own time: 11.3 us -> 0 us
    dot_general x42 -> x0, matrix products: 174 us -> none  [the longest x8 54.2 us: add_tiles(): jnp.einsum('gtb,rgtkhd->rbkhd', onehot, high_part, preferred_element_type...]
    unnamed x31 -> x5, local copies, waits for them, and re-layouts: 92 us -> 0.68 us
    pallas_call x0 -> x5, Pallas kernels: none -> 79.6 us  [the longest x2 56 us: attend(): pl.pallas_call(functools.partial(attend_kernel, heads, block_total, slots...]
    unnamed x6 -> x0, other arithmetic: 66.3 us -> none
    another operation x8 -> x0, local copies, waits for them, and re-layouts: 63.1 us -> none
    another operation x20 -> x0, other arithmetic: 46 us -> none
    all_to_all x0 -> x1, blocking collectives: none -> 42.3 us  [per_device(): lax.all_to_all(grads, 'seq', split_axis=0, concat_axis=0, tiled=True)]
    convert_element_type x10 -> x0, local copies, waits for them, and re-layouts: 37.4 us -> none  [the longest x2 14.9 us: per_device(): grad_keys.reshape(flat_shape).astype(jnp.bfloat16)]
  transfers between devices with their start and end apart: 7 -> 3, of which waited for: 3 -> 3; matrix products, arithmetic and copies ran while one was open for 21% -> 0% of each run, Pallas kernels for 0% -> 30%
where the time goes in v1:
time: 213 us; the launch traced here: 212 us
  Pallas kernels  79.6 us (37%)
  waiting for transfers between devices  71.7 us (34%)
  blocking collectives  42.3 us (20%)
  starting transfers between devices  13.2 us (6%)
  other arithmetic  2.44 us (1%)
    all_to_all x2, waiting for transfers between devices, per_device(): lax.all_to_all(packed, 'seq', split_axis=0, concat_axis=0, tiled=True)  61.9 us
    pallas_call x2, Pallas kernels, attend(): pl.pallas_call(functools.partial(attend_kernel, heads, block_total, slots...  56 us
    all_to_all x1, blocking collectives, per_device(): lax.all_to_all(grads, 'seq', split_axis=0, concat_axis=0, tiled=True)  42.3 us
    pallas_call x2, Pallas kernels, pack(): pl.pallas_call(functools.partial(pack_kernel, heads), grid_spec=pltpu.Pre...  15.5 us
    all_to_all x1, waiting for transfers between devices, per_device(): lax.all_to_all(grads, 'seq', split_axis=0, concat_axis=0, tiled=True)  9.79 us
    all_to_all x2, starting transfers between devices, per_device(): lax.all_to_all(packed, 'seq', split_axis=0, concat_axis=0, tiled=True)  9.53 us
    pallas_call x1, Pallas kernels, unpack(): pl.pallas_call(functools.partial(unpack_kernel, heads), grid=(devices,),...  8.03 us
  transfers between devices with their start and end apart: 3, of which 3 were waited for; matrix products, arithmetic and copies ran while one was open for 0% of the time, Pallas kernels for 30%

profile of v1, /device:TPU:0, one launch (start us, length us, event | category | flops | bytes accessed | tf_op | source)
XLA Modules:
  0.0 211.8 jit_solution(9698688289153237942)
XLA Ops:
  1.9 1.9 convert_element_type.3.table_ref
  3.8 0.6 pad_add_fusion.spot_ref
  4.4 7.7 %pack.3 = bf16[8,4,2,256,128]{4,3,2,1,0:T(8,128)(2,1)} custom-call(s32[2]{0:T(128)} %pad_add_fusion.spot_ref, bf16[256,4096]{1,0:T(8,128)(2,1)} %q_ref.3, bf16[256,4096]{1,0:T(8,128)(2,1)} %k_ref.3, bf16[256,4096]{1,0:T(8,128)(2,1)} %v_ref.3, bf16[1,256,4096]{2,1,0:T(8,128)(2,1)} %g_ref.3, f32[33,4096]{1,0:T(8,128)} %convert_element_type.3.table_ref), custom_call_target="tpu_custom_call" | custom-call | bytes 8388608 | tf_op jit(solution)/shard_map/pack/pallas_call | solution.py:41
  12.1 5.0 %all-to-all-start.2 = ((bf16[8,4,2,256,128]{4,3,2,1,0:T(8,128)(2,1)}), bf16[8,4,2,256,128]{4,3,2,1,0:T(8,128)(2,1)}, u32[]{:S(2)}, u32[]{:S(2)}) async-start(bf16[8,4,2,256,128]{4,3,2,1,0:T(8,128)(2,1)} %pack.3), calls=%async_computation.2 | async-start | bytes 8388608 | tf_op jit(solution)/shard_map/all_to_all | solution.py:199
  17.1 7.8 %pack.2 = bf16[8,4,2,256,128]{4,3,2,1,0:T(8,128)(2,1)} custom-call(s32[2]{0:T(128)} %pad_add_fusion.spot_ref, bf16[256,4096]{1,0:T(8,128)(2,1)} %q_ref.3, bf16[256,4096]{1,0:T(8,128)(2,1)} %k_ref.3, bf16[256,4096]{1,0:T(8,128)(2,1)} %v_ref.3, bf16[1,256,4096]{2,1,0:T(8,128)(2,1)} %g_ref.3, f32[33,4096]{1,0:T(8,128)} %convert_element_type.3.table_ref), custom_call_target="tpu_custom_call" | custom-call | bytes 8388608 | tf_op jit(solution)/shard_map/pack/pallas_call | solution.py:41
  24.9 0.0 copy-start.1
  24.9 41.4 %all-to-all-done.2.x_ref = bf16[8,4,2,256,128]{4,3,2,1,0:T(8,128)(2,1)} async-done(((bf16[8,4,2,256,128]{4,3,2,1,0:T(8,128)(2,1)}), bf16[8,4,2,256,128]{4,3,2,1,0:T(8,128)(2,1)}, u32[]{:S(2)}, u32[]{:S(2)}) %all-to-all-start.2) | async-done | bytes 4194336 | tf_op jit(solution)/shard_map/all_to_all | solution.py:199
  66.3 4.5 %all-to-all-start = ((bf16[8,4,2,256,128]{4,3,2,1,0:T(8,128)(2,1)}), bf16[8,4,2,256,128]{4,3,2,1,0:T(8,128)(2,1)}, u32[]{:S(2)}, u32[]{:S(2)}) async-start(bf16[8,4,2,256,128]{4,3,2,1,0:T(8,128)(2,1)} %pack.2), calls=%async_computation | async-start | bytes 8388608 | tf_op jit(solution)/shard_map/all_to_all | solution.py:199
  70.9 0.0 copy-done.1
  70.9 0.7 copy.12.tiles_ref
  71.6 28.0 %attend.3 = bf16[8,3,2,256,128]{4,3,2,1,0:T(8,128)(2,1)} custom-call(s32[16,8]{1,0:T(8,128)} %copy.12.tiles_ref, s32[16]{0:T(128)} %counts_ref.3, bf16[8,4,2,256,128]{4,3,2,1,0:T(8,128)(2,1)} %all-to-all-done.2.x_ref), custom_call_target="tpu_custom_call" | custom-call | flops 21474836480 | bytes 7340032 | tf_op jit(solution)/shard_map/attend/pallas_call | solution.py:146
  99.5 20.5 %all-to-all-done.x_ref = bf16[8,4,2,256,128]{4,3,2,1,0:T(8,128)(2,1)} async-done(((bf16[8,4,2,256,128]{4,3,2,1,0:T(8,128)(2,1)}), bf16[8,4,2,256,128]{4,3,2,1,0:T(8,128)(2,1)}, u32[]{:S(2)}, u32[]{:S(2)}) %all-to-all-start) | async-done | bytes 4194336 | tf_op jit(solution)/shard_map/all_to_all | solution.py:199
  120.0 3.6 %all-to-all-start.3 = ((bf16[8,3,2,256,128]{4,3,2,1,0:T(8,128)(2,1)}), bf16[8,3,2,256,128]{4,3,2,1,0:T(8,128)(2,1)S(1)}, u32[]{:S(2)}, u32[]{:S(2)}) async-start(bf16[8,3,2,256,128]{4,3,2,1,0:T(8,128)(2,1)} %attend.3), calls=%async_computation.3 | async-start | bytes 6291456 | tf_op jit(solution)/shard_map/all_to_all | solution.py:203
  123.7 28.0 %attend.2 = bf16[8,3,2,256,128]{4,3,2,1,0:T(8,128)(2,1)} custom-call(s32[16,8]{1,0:T(8,128)} %copy.12.tiles_ref, s32[16]{0:T(128)} %counts_ref.3, bf16[8,4,2,256,128]{4,3,2,1,0:T(8,128)(2,1)} %all-to-all-done.x_ref), custom_call_target="tpu_custom_call" | custom-call | flops 21474836480 | bytes 7340032 | tf_op jit(solution)/shard_map/attend/pallas_call | solution.py:146
  151.7 9.8 %all-to-all-done.3.refs_1_ = bf16[8,3,2,256,128]{4,3,2,1,0:T(8,128)(2,1)S(1)} async-done(((bf16[8,3,2,256,128]{4,3,2,1,0:T(8,128)(2,1)}), bf16[8,3,2,256,128]{4,3,2,1,0:T(8,128)(2,1)S(1)}, u32[]{:S(2)}, u32[]{:S(2)}) %all-to-all-start.3) | async-done | bytes 3145760 | tf_op jit(solution)/shard_map/all_to_all | solution.py:203
  161.5 0.0 copy-start
  161.5 42.3 %all_to_all.20.refs_0_ = bf16[8,3,2,256,128]{4,3,2,1,0:T(8,128)(2,1)} all-to-all(bf16[8,3,2,256,128]{4,3,2,1,0:T(8,128)(2,1)} %attend.2), channel_id=1, replica_groups=mesh['rows'=4,'seq'=8] {'seq'}, dimensions={0} | all-to-all | bytes 6291456 | tf_op jit(solution)/shard_map/all_to_all | solution.py:203
  203.7 0.0 copy-done
  203.7 8.0 %unpack.1 = (bf16[1,256,4096]{2,1,0:T(8,128)(2,1)}, bf16[1,256,4096]{2,1,0:T(8,128)(2,1)}, bf16[1,256,4096]{2,1,0:T(8,128)(2,1)}) custom-call(bf16[8,3,2,256,128]{4,3,2,1,0:T(8,128)(2,1)} %all_to_all.20.refs_0_, bf16[8,3,2,256,128]{4,3,2,1,0:T(8,128)(2,1)} %copy-done), custom_call_target="tpu_custom_call" | custom-call | tf_op jit(solution)/shard_map/unpack/pallas_call | solution.py:179
Async XLA Ops:
  12.1 54.2 %all-to-all-start.2 = ((bf16[8,4,2,256,128]{4,3,2,1,0:T(8,128)(2,1)}), bf16[8,4,2,256,128]{4,3,2,1,0:T(8,128)(2,1)}, u32[]{:S(2)}, u32[]{:S(2)}) async-start(bf16[8,4,2,256,128]{4,3,2,1,0:T(8,128)(2,1)} %pack.3), calls=%async_computation.2 | async-start | bytes 8388608 | tf_op jit(solution)/shard_map/all_to_all | solution.py:199
  24.9 46.0 %copy-start.1 = (s32[16,8]{0,1:T(8,128)S(1)}, s32[16,8]{0,1:T(8,128)}, u32[]{:S(2)}) copy-start(s32[16,8]{0,1:T(8,128)} %param.16) | copy-start | bytes 1540
  66.3 53.7 %all-to-all-start = ((bf16[8,4,2,256,128]{4,3,2,1,0:T(8,128)(2,1)}), bf16[8,4,2,256,128]{4,3,2,1,0:T(8,128)(2,1)}, u32[]{:S(2)}, u32[]{:S(2)}) async-start(bf16[8,4,2,256,128]{4,3,2,1,0:T(8,128)(2,1)} %pack.2), calls=%async_computation | async-start | bytes 8388608 | tf_op jit(solution)/shard_map/all_to_all | solution.py:199
  120.0 41.5 %all-to-all-start.3 = ((bf16[8,3,2,256,128]{4,3,2,1,0:T(8,128)(2,1)}), bf16[8,3,2,256,128]{4,3,2,1,0:T(8,128)(2,1)S(1)}, u32[]{:S(2)}, u32[]{:S(2)}) async-start(bf16[8,3,2,256,128]{4,3,2,1,0:T(8,128)(2,1)} %attend.3), calls=%async_computation.3 | async-start | bytes 6291456 | tf_op jit(solution)/shard_map/all_to_all | solution.py:203
  161.5 42.3 %copy-start = (bf16[8,3,2,256,128]{4,3,2,1,0:T(8,128)(2,1)}, bf16[8,3,2,256,128]{4,3,2,1,0:T(8,128)(2,1)S(1)}, u32[]{:S(2)}) copy-start(bf16[8,3,2,256,128]{4,3,2,1,0:T(8,128)(2,1)S(1)} %all-to-all-done.3.refs_1_) | copy-start | bytes 9437188

commit v2 on v0

v2 whole, which is shorter than its diff:
```python
import functools

import jax
import jax.numpy as jnp
from jax import lax
from jax.experimental import pallas as pl
from jax.experimental.pallas import tpu as pltpu
from jax.sharding import PartitionSpec as P

D_HEAD = 128
BLOCK = 128
NEG = -1e30
LOG2E = 1.4426950408889634
VMEM_LIMIT = 60 * 1024 * 1024
MESH = pl.DeviceIdType.MESH


def fused_kernel(
    n,
    heads,
    pos_ref,
    bias_ref,
    added_ref,
    q_hbm,
    k_hbm,
    v_hbm,
    g_hbm,
    gq_hbm,
    gk_hbm,
    gv_hbm,
    recv,
    outs,
    kt_ref,
    s_ref,
    w_ref,
    dp_ref,
    dk_ref,
    dv_ref,
    in_send,
    in_recv,
    in_local,
    out_send,
    out_recv,
    out_local,
):
    me = lax.axis_index("seq")
    tok = q_hbm.shape[0]
    per = tok // BLOCK
    scale = D_HEAD ** (-0.5)
    nt = (((1,), (1,)), ((), ()))
    nn = (((1,), (0,)), ((), ()))
    results = (gq_hbm, gk_hbm, gv_hbm)

    def peer(step):
        return lax.rem(me + step, n)

    barrier = pltpu.get_barrier_semaphore()

    def greet(step, carry):
        pl.semaphore_signal(barrier, inc=1, device_id={"seq": peer(step)}, device_id_type=MESH)
        return carry

    lax.fori_loop(1, n, greet, 0)
    pl.semaphore_wait(barrier, n - 1)

    def columns(owner, h):
        return pl.ds(pl.multiple_of((owner * heads + h) * D_HEAD, D_HEAD), D_HEAD)

    def sources(cols):
        return (q_hbm.at[:, cols], k_hbm.at[:, cols], v_hbm.at[:, cols], g_hbm.at[0, :, cols])

    def send_in(h):
        def one(step, carry):
            to = peer(step)
            for a, src in enumerate(sources(columns(to, h))):
                pltpu.make_async_remote_copy(
                    src_ref=src,
                    dst_ref=recv.at[h, me, a],
                    send_sem=in_send.at[h],
                    recv_sem=in_recv.at[h],
                    device_id={"seq": to},
                    device_id_type=MESH,
                ).start()
            return carry

        lax.fori_loop(1, n, one, 0)
        for a, src in enumerate(sources(columns(me, h))):
            pltpu.make_async_copy(src, recv.at[h, me, a], in_local.at[h]).start()

    def wait_bytes(ref, sem):
        pltpu.make_async_copy(ref, ref, sem).wait()

    def wait_sent(h):
        wait_bytes(recv.at[h, pl.ds(0, n - 1)], in_send.at[h])

    def wait_in(h):
        wait_bytes(recv.at[h, pl.ds(0, n - 1)], in_recv.at[h])
        wait_bytes(recv.at[h, 0], in_local.at[h])

    def send_out(h):
        cols = columns(me, h)

        def one(step, carry):
            to = peer(step)
            for a, dst in enumerate(results):
                pltpu.make_async_remote_copy(
                    src_ref=outs.at[h, to, a],
                    dst_ref=dst.at[0, :, cols],
                    send_sem=out_send,
                    recv_sem=out_recv,
                    device_id={"seq": to},
                    device_id_type=MESH,
                ).start()
            return carry

        lax.fori_loop(1, n, one, 0)
        for a, dst in enumerate(results):
            pltpu.make_async_copy(outs.at[h, me, a], dst.at[0, :, cols], out_local).start()

    def attend(h):
        def turn(src, carry):
            kt_ref[src] = recv[h, src, 1].astype(jnp.float32).T.astype(jnp.bfloat16)
            return carry

        lax.fori_loop(0, n, turn, 0)
        dk_ref[...] = jnp.zeros_like(dk_ref)
        dv_ref[...] = jnp.zeros_like(dv_ref)
        added = added_ref[pl.ds(h, 1), :]

        def queries_of(src, carry):
            q = recv[h, src, 0]
            at = lax.broadcasted_iota(jnp.int32, (tok, D_HEAD), 0) + src * tok
            term = jnp.where(at == pos_ref[0], added, 0.0)
            cot = (recv[h, src, 3].astype(jnp.float32) + term).astype(jnp.bfloat16)
            top = jnp.full((1, tok), NEG, jnp.float32)
            for c in range(n):
                scores = lax.dot_general(recv[h, c, 1], q, nt, preferred_element_type=jnp.float32)
                for b in range(per):
                    part = scores[b * BLOCK : (b + 1) * BLOCK] + bias_ref[src, pl.ds(c * per + b, 1), :]
                    s_ref[c, b * BLOCK : (b + 1) * BLOCK, :] = part
                    top = jnp.maximum(top, jnp.max(part, axis=0, keepdims=True))
            total = jnp.zeros((1, tok), jnp.float32)
            delta = jnp.zeros((1, tok), jnp.float32)
            for c in range(n):
                weights = jnp.exp2((s_ref[c] - top) * (scale * LOG2E))
                grad_probs = lax.dot_general(
                    recv[h, c, 2], cot, nt, preferred_element_type=jnp.float32
                )
                w_ref[c] = weights
                dp_ref[c] = grad_probs
                total += jnp.sum(weights, axis=0, keepdims=True)
                delta += jnp.sum(weights * grad_probs, axis=0, keepdims=True)
            inverse = 1.0 / total
            delta = delta * inverse
            query_t = jnp.zeros((D_HEAD, tok), jnp.float32)
            for c in range(n):
                probs = w_ref[c] * inverse
                grad_scores = (probs * (dp_ref[c] - delta)).astype(jnp.bfloat16)
                dv_ref[c] += lax.dot_general(
                    probs.astype(jnp.bfloat16), cot, nn, preferred_element_type=jnp.float32
                )
                dk_ref[c] += lax.dot_general(grad_scores, q, nn, preferred_element_type=jnp.float32)
                query_t += lax.dot_general(
                    kt_ref[c], grad_scores, nn, preferred_element_type=jnp.float32
                )
            outs[h, src, 0] = (scale * query_t.T).astype(jnp.bfloat16)
            return carry

        lax.fori_loop(0, n, queries_of, 0)

        def close(src, carry):
            outs[h, src, 1] = (scale * dk_ref[src]).astype(jnp.bfloat16)
            outs[h, src, 2] = dv_ref[src].astype(jnp.bfloat16)
            return carry

        lax.fori_loop(0, n, close, 0)

    send_in(0)
    wait_sent(0)
    if heads > 1:
        send_in(1)

    def turn_of(h, carry):
        wait_in(h)

        @pl.when(h + 2 < heads)
        def ahead():
            send_in(h + 2)

        attend(h)
        send_out(h)
        return carry

    lax.fori_loop(0, heads, turn_of, 0)
    for h in range(1, heads):
        wait_sent(h)
    wait_bytes(outs.at[:, pl.ds(0, n - 1)], out_send)
    wait_bytes(outs.at[:, pl.ds(0, n - 1)], out_recv)
    wait_bytes(outs.at[:, 0], out_local)


def per_device(queries, keys, values, grad_out, table, positions, residues, tiles, counts):
    n = lax.axis_size("seq")
    tok, width = queries.shape
    heads = width // D_HEAD // n
    block_total, slots = tiles.shape
    used = jnp.arange(slots, dtype=jnp.int32)[None, :] < counts[:, None]
    blocks = jnp.arange(block_total, dtype=jnp.int32)
    listed = jnp.any((tiles[:, :, None] == blocks) & used[:, :, None], axis=1)
    bias = jnp.where(listed, 0.0, NEG).astype(jnp.float32)
    bias = bias.reshape(n, tok // BLOCK, block_total).transpose(0, 2, 1)
    bias = jnp.repeat(bias, BLOCK, axis=2)
    own = lax.dynamic_slice(
        table, (residues[0], lax.axis_index("seq") * heads * D_HEAD), (1, heads * D_HEAD)
    )
    added = own.astype(jnp.float32).reshape(heads, D_HEAD)
    hbm = pl.BlockSpec(memory_space=pl.ANY)
    vmem = pl.BlockSpec(memory_space=pltpu.VMEM)
    shape = jax.ShapeDtypeStruct((1, tok, width), jnp.bfloat16)
    return pl.pallas_call(
        functools.partial(fused_kernel, n, heads),
        in_specs=[pl.BlockSpec(memory_space=pltpu.SMEM), vmem, vmem, hbm, hbm, hbm, hbm],
        out_specs=[hbm] * 3,
        out_shape=[shape] * 3,
        scratch_shapes=[
            pltpu.VMEM((heads, n, 4, tok, D_HEAD), jnp.bfloat16),
            pltpu.VMEM((heads, n, 3, tok, D_HEAD), jnp.bfloat16),
            pltpu.VMEM((n, D_HEAD, tok), jnp.bfloat16),
            pltpu.VMEM((n, tok, tok), jnp.float32),
            pltpu.VMEM((n, tok, tok), jnp.float32),
            pltpu.VMEM((n, tok, tok), jnp.float32),
            pltpu.VMEM((n, tok, D_HEAD), jnp.float32),
            pltpu.VMEM((n, tok, D_HEAD), jnp.float32),
            pltpu.SemaphoreType.DMA((heads,)),
            pltpu.SemaphoreType.DMA((heads,)),
            pltpu.SemaphoreType.DMA((heads,)),
            pltpu.SemaphoreType.DMA,
            pltpu.SemaphoreType.DMA,
            pltpu.SemaphoreType.DMA,
        ],
        compiler_params=pltpu.CompilerParams(
            vmem_limit_bytes=VMEM_LIMIT, collective_id=0, has_side_effects=True
        ),
        name="fused",
    )(positions, bias, added, queries, keys, values, grad_out)


def solution(mesh):
    placed = (
        P("seq", None),
        P("seq", None),
        P("seq", None),
        P("rows", "seq", None),
        P(),
        P("rows"),
        P("rows"),
        P(),
        P(),
    )
    return jax.shard_map(
        per_device,
        mesh=mesh,
        in_specs=placed,
        out_specs=(P("rows", "seq", None), P("rows", "seq", None), P("rows", "seq", None)),
        check_vma=False,
    )
```

time: 699 us -> 177 us (0.25); the launches traced: 690 us -> 177 us
  local copies, waits for them, and re-layouts: 255 us -> 8.79 us
  matrix products: 186 us -> 0 us
  Pallas kernels: 0 us -> 164 us
  other arithmetic: 122 us -> 2.21 us
  waiting for transfers between devices: 67.7 us -> 0 us
  starting transfers between devices: 31.6 us -> 0 us
  blocking collectives: 13.4 us -> 0 us
  loops' own time: 11.3 us -> 0 us
    dot_general x42 -> x0, matrix products: 174 us -> none  [the longest x8 54.2 us: add_tiles(): jnp.einsum('gtb,rgtkhd->rbkhd', onehot, high_part, preferred_element_type...]
    pallas_call x0 -> x1, Pallas kernels: none -> 164 us  [per_device(): pl.pallas_call(functools.partial(fused_kernel, n, heads), in_specs=[pl.Bl...]
    unnamed x31 -> x8, local copies, waits for them, and re-layouts: 92 us -> 7.71 us
    all_to_all x7 -> x0, waiting for transfers between devices: 67.7 us -> none  [the longest x1 22.6 us: per_device(): lax.all_to_all(queries, 'seq', split_axis=1, concat_axis=0, tiled=True)]
    unnamed x6 -> x0, other arithmetic: 66.3 us -> none
    another operation x8 -> x0, local copies, waits for them, and re-layouts: 63.1 us -> none
    another operation x20 -> x0, other arithmetic: 46 us -> none
    convert_element_type x10 -> x0, local copies, waits for them, and re-layouts: 37.4 us -> none  [the longest x2 14.9 us: per_device(): grad_keys.reshape(flat_shape).astype(jnp.bfloat16)]
  transfers between devices with their start and end apart: 7 -> 0, of which waited for: 3 -> 0; matrix products, arithmetic and copies ran while one was open for 21% -> 0% of each run, Pallas kernels for 0% -> 0%
where the time goes in v2:
time: 177 us
  Pallas kernels  164 us (93%)
  local copies, waits for them, and re-layouts  8.79 us (5%)
  other arithmetic  2.21 us (1%)
  between operations  1.96 us (1%)
    pallas_call x1, Pallas kernels, per_device(): pl.pallas_call(functools.partial(fused_kernel, n, heads), in_specs=[pl.Bl...  164 us
    unnamed x8, local copies, waits for them, and re-layouts  7.71 us

profile of v2, /device:TPU:0, one launch (start us, length us, event | category | flops | bytes accessed | tf_op | source)
XLA Modules:
  0.0 177.0 jit_solution(14694966571133408473)
XLA Ops:
  1.9 1.4 dynamic-slice_convert_fusion
  3.3 0.7 iota_compare_fusion.1
  4.0 0.8 copy.15
  4.8 0.1 fusion.1
  4.9 0.1 copy.16
  5.0 0.2 broadcast_in_dim.18
  5.2 0.8 reshape.41.bias_ref
  6.0 164.0 %fused.1 = (bf16[1,256,4096]{2,1,0:T(8,128)(2,1)}, bf16[1,256,4096]{2,1,0:T(8,128)(2,1)}, bf16[1,256,4096]{2,1,0:T(8,128)(2,1)}) custom-call(s32[1]{0:T(128)S(6)} %copy.20.pos_ref, f32[8,16,256]{2,1,0:T(8,128)} %reshape.41.bias_ref, f32[4,128]{1,0:T(4,128)} %bitcast.9, bf16[256,4096]{1,0:T(8,128)(2,1)} %q_hbm.1, bf16[256,4096]{1,0:T(8,128)(2,1)} %k_hbm.1, ...), custom_call_target="tpu_custom_call" | custom-call | tf_op jit(solution)/shard_map/fused/pallas_call | solution.py:220
  170.0 0.0 copy-start.1
  170.0 3.3 %copy.22 = bf16[1,256,4096]{2,1,0:T(8,128)(2,1)} copy(bf16[1,256,4096]{2,1,0:T(8,128)(2,1)} %get-tuple-element.6) | data formatting | bytes 4194304
  173.3 0.0 copy-done.1
  173.3 0.0 copy-start
  173.3 1.3 copy.23
  174.6 1.0 copy-done
  175.7 1.3 copy.24
  (1 shorter events, 0.0 us)
Async XLA Ops:
  170.0 3.3 %copy-start.1 = (bf16[1,256,4096]{2,1,0:T(8,128)(2,1)S(1)}, bf16[1,256,4096]{2,1,0:T(8,128)(2,1)}, u32[]{:S(2)}) copy-start(bf16[1,256,4096]{2,1,0:T(8,128)(2,1)} %get-tuple-element.7) | copy-start | bytes 6291460
  173.3 2.3 %copy-start = (bf16[1,256,4096]{2,1,0:T(8,128)(2,1)S(1)}, bf16[1,256,4096]{2,1,0:T(8,128)(2,1)}, u32[]{:S(2)}) copy-start(bf16[1,256,4096]{2,1,0:T(8,128)(2,1)} %get-tuple-element.8) | copy-start | bytes 6291460

commit v3 on v2

--- a/solution.py
+++ b/solution.py
@@ -19,8 +19,10 @@
     n,
     heads,
     pos_ref,
-    bias_ref,
-    added_ref,
+    residue_ref,
+    tiles_ref,
+    counts_ref,
+    table_ref,
     q_hbm,
     k_hbm,
     v_hbm,
@@ -30,10 +32,11 @@
     gv_hbm,
     recv,
     outs,
+    bias_ref,
     kt_ref,
+    vt_ref,
     s_ref,
     w_ref,
-    dp_ref,
     dk_ref,
     dv_ref,
     in_send,
@@ -119,13 +122,16 @@
 
     def attend(h):
         def turn(src, carry):
-            kt_ref[src] = recv[h, src, 1].astype(jnp.float32).T.astype(jnp.bfloat16)
+            kt_ref[src] = recv[h, src, 1].T
+            vt_ref[src] = recv[h, src, 2].T
             return carry
 
         lax.fori_loop(0, n, turn, 0)
         dk_ref[...] = jnp.zeros_like(dk_ref)
         dv_ref[...] = jnp.zeros_like(dv_ref)
-        added = added_ref[pl.ds(h, 1), :]
+        rows = table_ref[:, columns(me, h)].astype(jnp.float32)
+        picked = lax.broadcasted_iota(jnp.int32, rows.shape, 0) == residue_ref[0]
+        added = jnp.sum(jnp.where(picked, rows, 0.0), axis=0, keepdims=True)
 
         def queries_of(src, carry):
             q = recv[h, src, 0]
@@ -140,24 +146,29 @@
                     s_ref[c, b * BLOCK : (b + 1) * BLOCK, :] = part
                     top = jnp.maximum(top, jnp.max(part, axis=0, keepdims=True))
             total = jnp.zeros((1, tok), jnp.float32)
-            delta = jnp.zeros((1, tok), jnp.float32)
+            attended = jnp.zeros((D_HEAD, tok), jnp.float32)
             for c in range(n):
                 weights = jnp.exp2((s_ref[c] - top) * (scale * LOG2E))
-                grad_probs = lax.dot_general(
-                    recv[h, c, 2], cot, nt, preferred_element_type=jnp.float32
-                )
-                w_ref[c] = weights
-                dp_ref[c] = grad_probs
                 total += jnp.sum(weights, axis=0, keepdims=True)
-                delta += jnp.sum(weights * grad_probs, axis=0, keepdims=True)
+                weights_bf = weights.astype(jnp.bfloat16)
+                w_ref[c] = weights_bf
+                attended += lax.dot_general(
+                    vt_ref[c], weights_bf, nn, preferred_element_type=jnp.float32
+                )
             inverse = 1.0 / total
-            delta = delta * inverse
+            cot_t = (cot.astype(jnp.float32).T * inverse).astype(jnp.bfloat16)
+            cot_wide = cot_t.astype(jnp.float32)
+            scaled = cot_wide.T.astype(jnp.bfloat16)
+            delta = inverse * jnp.sum(cot_wide * attended, axis=0, keepdims=True)
             query_t = jnp.zeros((D_HEAD, tok), jnp.float32)
             for c in range(n):
-                probs = w_ref[c] * inverse
-                grad_scores = (probs * (dp_ref[c] - delta)).astype(jnp.bfloat16)
+                grad_probs = lax.dot_general(
+                    recv[h, c, 2], cot_t, nn, preferred_element_type=jnp.float32
+                )
+                weights_bf = w_ref[c]
+                grad_scores = weights_bf * (grad_probs - delta).astype(jnp.bfloat16)
                 dv_ref[c] += lax.dot_general(
-                    probs.astype(jnp.bfloat16), cot, nn, preferred_element_type=jnp.float32
+                    weights_bf, scaled, nn, preferred_element_type=jnp.float32
                 )
                 dk_ref[c] += lax.dot_general(grad_scores, q, nn, preferred_element_type=jnp.float32)
                 query_t += lax.dot_general(
@@ -175,7 +186,18 @@
 
         lax.fori_loop(0, n, close, 0)
 
+    def mask_of(src, carry):
+        for p in range(per):
+            block = src * per + p
+            ids = lax.broadcasted_iota(jnp.int32, (bias_ref.shape[1], BLOCK), 0)
+            hit = ids == tiles_ref[block, 0]
+            for j in range(1, tiles_ref.shape[1]):
+                hit |= ids == jnp.where(j < counts_ref[block], tiles_ref[block, j], -1)
+            bias_ref[src, :, p * BLOCK : (p + 1) * BLOCK] = jnp.where(hit, 0.0, NEG)
+        return carry
+
     send_in(0)
+    lax.fori_loop(0, n, mask_of, 0)
     wait_sent(0)
     if heads > 1:
         send_in(1)
@@ -203,32 +225,24 @@
     n = lax.axis_size("seq")
     tok, width = queries.shape
     heads = width // D_HEAD // n
-    block_total, slots = tiles.shape
-    used = jnp.arange(slots, dtype=jnp.int32)[None, :] < counts[:, None]
-    blocks = jnp.arange(block_total, dtype=jnp.int32)
-    listed = jnp.any((tiles[:, :, None] == blocks) & used[:, :, None], axis=1)
-    bias = jnp.where(listed, 0.0, NEG).astype(jnp.float32)
-    bias = bias.reshape(n, tok // BLOCK, block_total).transpose(0, 2, 1)
-    bias = jnp.repeat(bias, BLOCK, axis=2)
-    own = lax.dynamic_slice(
-        table, (residues[0], lax.axis_index("seq") * heads * D_HEAD), (1, heads * D_HEAD)
-    )
-    added = own.astype(jnp.float32).reshape(heads, D_HEAD)
+    block_total = tiles.shape[0]
     hbm = pl.BlockSpec(memory_space=pl.ANY)
+    smem = pl.BlockSpec(memory_space=pltpu.SMEM)
     vmem = pl.BlockSpec(memory_space=pltpu.VMEM)
     shape = jax.ShapeDtypeStruct((1, tok, width), jnp.bfloat16)
     return pl.pallas_call(
         functools.partial(fused_kernel, n, heads),
-        in_specs=[pl.BlockSpec(memory_space=pltpu.SMEM), vmem, vmem, hbm, hbm, hbm, hbm],
+        in_specs=[smem, smem, smem, smem, vmem, hbm, hbm, hbm, hbm],
         out_specs=[hbm] * 3,
         out_shape=[shape] * 3,
         scratch_shapes=[
             pltpu.VMEM((heads, n, 4, tok, D_HEAD), jnp.bfloat16),
             pltpu.VMEM((heads, n, 3, tok, D_HEAD), jnp.bfloat16),
+            pltpu.VMEM((n, block_total, tok), jnp.float32),
+            pltpu.VMEM((n, D_HEAD, tok), jnp.bfloat16),
             pltpu.VMEM((n, D_HEAD, tok), jnp.bfloat16),
             pltpu.VMEM((n, tok, tok), jnp.float32),
-            pltpu.VMEM((n, tok, tok), jnp.float32),
-            pltpu.VMEM((n, tok, tok), jnp.float32),
+            pltpu.VMEM((n, tok, tok), jnp.bfloat16),
             pltpu.VMEM((n, tok, D_HEAD), jnp.float32),
             pltpu.VMEM((n, tok, D_HEAD), jnp.float32),
             pltpu.SemaphoreType.DMA((heads,)),
@@ -242,7 +256,7 @@
             vmem_limit_bytes=VMEM_LIMIT, collective_id=0, has_side_effects=True
         ),
         name="fused",
-    )(positions, bias, added, queries, keys, values, grad_out)
+    )(positions, residues, tiles, counts, table, queries, keys, values, grad_out)
 
 
 def solution(mesh):

time: 177 us -> 175 us (0.989)
  other arithmetic: 2.21 us -> 0 us
where the time goes in v3:
time: 175 us; the launch traced here: 174 us
  Pallas kernels  164 us (94%)
  local copies, waits for them, and re-layouts  8.3 us (5%)
  between operations  1.94 us (1%)
    pallas_call x1, Pallas kernels, per_device(): pl.pallas_call(functools.partial(fused_kernel, n, heads), in_specs=[smem,...  164 us
    unnamed x8, local copies, waits for them, and re-layouts  8.3 us

profile of v3, /device:TPU:0, one launch (start us, length us, event | category | flops | bytes accessed | tf_op | source)
XLA Modules:
  0.0 174.3 jit_solution(11031715978307371297)
XLA Ops:
  1.9 1.4 copy.12.tiles_ref
  3.3 164.1 %fused.1 = (bf16[1,256,4096]{2,1,0:T(8,128)(2,1)}, bf16[1,256,4096]{2,1,0:T(8,128)(2,1)}, bf16[1,256,4096]{2,1,0:T(8,128)(2,1)}) custom-call(s32[1]{0:T(128)S(6)} %copy.16.pos_ref, s32[1]{0:T(128)S(6)} %copy.17.residue_ref, s32[16,8]{1,0:T(8,128)} %copy.12.tiles_ref, s32[16]{0:T(128)} %counts_ref.1, bf16[33,4096]{1,0:T(8,128)(2,1)} %table_ref.1, ...), custom_call_target="tpu_custom_call" | custom-call | tf_op jit(solution)/shard_map/fused/pallas_call | solution.py:233
  167.3 0.0 copy-start.1
  167.4 3.3 %copy.18 = bf16[1,256,4096]{2,1,0:T(8,128)(2,1)} copy(bf16[1,256,4096]{2,1,0:T(8,128)(2,1)} %get-tuple-element.6) | data formatting | bytes 4194304
  170.6 0.0 copy-done.1
  170.6 0.0 copy-start
  170.6 1.3 copy.19
  172.0 1.0 copy-done
  173.0 1.3 copy.20
Async XLA Ops:
  167.3 3.3 %copy-start.1 = (bf16[1,256,4096]{2,1,0:T(8,128)(2,1)S(1)}, bf16[1,256,4096]{2,1,0:T(8,128)(2,1)}, u32[]{:S(2)}) copy-start(bf16[1,256,4096]{2,1,0:T(8,128)(2,1)} %get-tuple-element.7) | copy-start | bytes 6291460
  170.6 2.3 %copy-start = (bf16[1,256,4096]{2,1,0:T(8,128)(2,1)S(1)}, bf16[1,256,4096]{2,1,0:T(8,128)(2,1)}, u32[]{:S(2)}) copy-start(bf16[1,256,4096]{2,1,0:T(8,128)(2,1)} %get-tuple-element.8) | copy-start | bytes 6291460

commit v4 on v3

--- a/solution.py
+++ b/solution.py
@@ -17,6 +17,7 @@
 
 def fused_kernel(
     n,
+    planes,
     heads,
     pos_ref,
     residue_ref,
@@ -42,6 +43,10 @@
     in_send,
     in_recv,
     in_local,
+    share_send,
+    share_recv,
+    plane_send,
+    plane_recv,
     out_send,
     out_recv,
     out_local,
@@ -54,8 +59,23 @@
     nn = (((1,), (0,)), ((), ()))
     results = (gq_hbm, gk_hbm, gv_hbm)
 
+    plane = lax.axis_index("rows")
+    share = tok // planes
+    own_rows = pl.ds(pl.multiple_of(plane * share, share), share)
+    core = lax.rem(me, 2)
+
     def peer(step):
-        return lax.rem(me + step, n)
+        high, mid, low = step // 4, (step // 2) % 2, step % 2
+        swapped = (high // 2) * 8 + mid * 4 + (high % 2) * 2 + low
+        off = step + core * (swapped - step)
+        return (
+            ((me // 4 + off // 4) % (n // 4)) * 4
+            + ((me // 2 + off // 2) % 2) * 2
+            + (me + off) % 2
+        )
+
+    def other_plane(step):
+        return lax.rem(plane + step, planes)
 
     barrier = pltpu.get_barrier_semaphore()
 
@@ -63,8 +83,14 @@
         pl.semaphore_signal(barrier, inc=1, device_id={"seq": peer(step)}, device_id_type=MESH)
         return carry
 
+    def greet_plane(step, carry):
+        to = other_plane(step)
+        pl.semaphore_signal(barrier, inc=1, device_id={"rows": to}, device_id_type=MESH)
+        return carry
+
     lax.fori_loop(1, n, greet, 0)
-    pl.semaphore_wait(barrier, n - 1)
+    lax.fori_loop(1, planes, greet_plane, 0)
+    pl.semaphore_wait(barrier, n - 1 + planes - 1)
 
     def columns(owner, h):
         return pl.ds(pl.multiple_of((owner * heads + h) * D_HEAD, D_HEAD), D_HEAD)
@@ -72,33 +98,79 @@
     def sources(cols):
         return (q_hbm.at[:, cols], k_hbm.at[:, cols], v_hbm.at[:, cols], g_hbm.at[0, :, cols])
 
-    def send_in(h):
+    def send_in(h, first):
         def one(step, carry):
             to = peer(step)
             for a, src in enumerate(sources(columns(to, h))):
+                if a >= first:
+                    pltpu.make_async_remote_copy(
+                        src_ref=src,
+                        dst_ref=recv.at[h, me, a],
+                        send_sem=in_send.at[h],
+                        recv_sem=in_recv.at[h],
+                        device_id={"seq": to},
+                        device_id_type=MESH,
+                    ).start()
+            return carry
+
+        lax.fori_loop(1, n, one, 0)
+        for a, src in enumerate(sources(columns(me, h))):
+            pltpu.make_async_copy(src, recv.at[h, me, a], in_local.at[h]).start()
+
+    def send_share(h):
+        def one(step, carry):
+            to = peer(step)
+            cols = columns(to, h)
+            for a, src in enumerate((q_hbm, k_hbm, v_hbm)):
                 pltpu.make_async_remote_copy(
-                    src_ref=src,
-                    dst_ref=recv.at[h, me, a],
-                    send_sem=in_send.at[h],
-                    recv_sem=in_recv.at[h],
+                    src_ref=src.at[own_rows, cols],
+                    dst_ref=recv.at[h, me, a, own_rows],
+                    send_sem=share_send.at[h],
+                    recv_sem=share_recv.at[h],
                     device_id={"seq": to},
                     device_id_type=MESH,
                 ).start()
             return carry
 
         lax.fori_loop(1, n, one, 0)
-        for a, src in enumerate(sources(columns(me, h))):
-            pltpu.make_async_copy(src, recv.at[h, me, a], in_local.at[h]).start()
+
+    def share_bytes(h):
+        return recv.at[h, pl.ds(0, n - 1), pl.ds(0, 3), pl.ds(0, share)]
+
+    def plane_bytes(h):
+        return recv.at[h, pl.ds(0, n - 1), pl.ds(0, 3), pl.ds(0, (planes - 1) * share)]
+
+    def forward(h):
+        wait_bytes(share_bytes(h), share_recv.at[h])
+
+        def one(step, carry):
+            block = recv.at[h, peer(step), pl.ds(0, 3), own_rows]
+
+            def over(hop, inner):
+                pltpu.make_async_remote_copy(
+                    src_ref=block,
+                    dst_ref=block,
+                    send_sem=plane_send.at[h],
+                    recv_sem=plane_recv.at[h],
+                    device_id={"rows": other_plane(hop)},
+                    device_id_type=MESH,
+                ).start()
+                return inner
+
+            return lax.fori_loop(1, planes, over, carry)
+
+        lax.fori_loop(1, n, one, 0)
 
     def wait_bytes(ref, sem):
         pltpu.make_async_copy(ref, ref, sem).wait()
 
     def wait_sent(h):
-        wait_bytes(recv.at[h, pl.ds(0, n - 1)], in_send.at[h])
-
-    def wait_in(h):
-        wait_bytes(recv.at[h, pl.ds(0, n - 1)], in_recv.at[h])
+        first = 0 if h == 0 else 3
+        wait_bytes(recv.at[h, pl.ds(0, n - 1), pl.ds(first, 4 - first)], in_send.at[h])
+
+    def wait_in(h, first):
         wait_bytes(recv.at[h, 0], in_local.at[h])
+        wait_bytes(recv.at[h, pl.ds(0, n - 1), pl.ds(first, 4 - first)], in_recv.at[h])
 
     def send_out(h):
         cols = columns(me, h)
@@ -134,6 +206,13 @@
         added = jnp.sum(jnp.where(picked, rows, 0.0), axis=0, keepdims=True)
 
         def queries_of(src, carry):
+            if heads > 2:
+
+                @pl.when((h == 0) & (src == min(3, n - 1)))
+                def onward():
+                    for later in range(2, heads):
+                        forward(later)
+
             q = recv[h, src, 0]
             at = lax.broadcasted_iota(jnp.int32, (tok, D_HEAD), 0) + src * tok
             term = jnp.where(at == pos_ref[0], added, 0.0)
@@ -196,18 +275,24 @@
             bias_ref[src, :, p * BLOCK : (p + 1) * BLOCK] = jnp.where(hit, 0.0, NEG)
         return carry
 
-    send_in(0)
+    if heads > 1:
+        send_share(1)
+    send_in(0, 0)
     lax.fori_loop(0, n, mask_of, 0)
+    if heads > 1:
+        forward(1)
     wait_sent(0)
-    if heads > 1:
-        send_in(1)
+    for h in range(2, heads):
+        send_share(h)
+    for h in range(1, heads):
+        send_in(h, 3)
+    wait_in(0, 0)
 
     def turn_of(h, carry):
-        wait_in(h)
-
-        @pl.when(h + 2 < heads)
-        def ahead():
-            send_in(h + 2)
+        @pl.when(h > 0)
+        def arrived():
+            wait_in(h, 3)
+            wait_bytes(plane_bytes(h), plane_recv.at[h])
 
         attend(h)
         send_out(h)
@@ -216,13 +301,15 @@
     lax.fori_loop(0, heads, turn_of, 0)
     for h in range(1, heads):
         wait_sent(h)
+        wait_bytes(share_bytes(h), share_send.at[h])
+        wait_bytes(plane_bytes(h), plane_send.at[h])
     wait_bytes(outs.at[:, pl.ds(0, n - 1)], out_send)
     wait_bytes(outs.at[:, pl.ds(0, n - 1)], out_recv)
     wait_bytes(outs.at[:, 0], out_local)
 
 
 def per_device(queries, keys, values, grad_out, table, positions, residues, tiles, counts):
-    n = lax.axis_size("seq")
+    n, planes = lax.axis_size("seq"), lax.axis_size("rows")
     tok, width = queries.shape
     heads = width // D_HEAD // n
     block_total = tiles.shape[0]
@@ -231,7 +318,7 @@
     vmem = pl.BlockSpec(memory_space=pltpu.VMEM)
     shape = jax.ShapeDtypeStruct((1, tok, width), jnp.bfloat16)
     return pl.pallas_call(
-        functools.partial(fused_kernel, n, heads),
+        functools.partial(fused_kernel, n, planes, heads),
         in_specs=[smem, smem, smem, smem, vmem, hbm, hbm, hbm, hbm],
         out_specs=[hbm] * 3,
         out_shape=[shape] * 3,
@@ -245,6 +332,10 @@
             pltpu.VMEM((n, tok, tok), jnp.bfloat16),
             pltpu.VMEM((n, tok, D_HEAD), jnp.float32),
             pltpu.VMEM((n, tok, D_HEAD), jnp.float32),
+            pltpu.SemaphoreType.DMA((heads,)),
+            pltpu.SemaphoreType.DMA((heads,)),
+            pltpu.SemaphoreType.DMA((heads,)),
+            pltpu.SemaphoreType.DMA((heads,)),
             pltpu.SemaphoreType.DMA((heads,)),
             pltpu.SemaphoreType.DMA((heads,)),
             pltpu.SemaphoreType.DMA((heads,)),

time: 175 us -> 161 us (0.920); the launches traced: 174 us -> 158 us
  Pallas kernels: 164 us -> 148 us
    pallas_call x1, Pallas kernels: 164 us -> 148 us  [per_device(): pl.pallas_call(functools.partial(fused_kernel, n, planes, heads), in_spec...]
where the time goes in v4:
time: 161 us; the launch traced here: 158 us
  Pallas kernels  148 us (92%)
  local copies, waits for them, and re-layouts  8.3 us (5%)
  between operations  1.94 us (1%)
    pallas_call x1, Pallas kernels, per_device(): pl.pallas_call(functools.partial(fused_kernel, n, planes, heads), in_spec...  148 us
    unnamed x8, local copies, waits for them, and re-layouts  8.3 us

profile of v4, /device:TPU:0, one launch (start us, length us, event | category | flops | bytes accessed | tf_op | source)
XLA Modules:
  0.0 158.1 jit_solution(933096955144908367)
XLA Ops:
  1.9 1.4 copy.12.tiles_ref
  3.3 147.9 %fused.1 = (bf16[1,256,4096]{2,1,0:T(8,128)(2,1)}, bf16[1,256,4096]{2,1,0:T(8,128)(2,1)}, bf16[1,256,4096]{2,1,0:T(8,128)(2,1)}) custom-call(s32[1]{0:T(128)S(6)} %copy.16.pos_ref, s32[1]{0:T(128)S(6)} %copy.17.residue_ref, s32[16,8]{1,0:T(8,128)} %copy.12.tiles_ref, s32[16]{0:T(128)} %counts_ref.1, bf16[33,4096]{1,0:T(8,128)(2,1)} %table_ref.1, ...), custom_call_target="tpu_custom_call" | custom-call | tf_op jit(solution)/shard_map/fused/pallas_call | solution.py:320
  151.1 0.0 copy-start.1
  151.2 3.3 %copy.18 = bf16[1,256,4096]{2,1,0:T(8,128)(2,1)} copy(bf16[1,256,4096]{2,1,0:T(8,128)(2,1)} %get-tuple-element.6) | data formatting | bytes 4194304
  154.4 0.0 copy-done.1
  154.4 0.0 copy-start
  154.4 1.3 copy.19
  155.8 1.0 copy-done
  156.8 1.3 copy.20
Async XLA Ops:
  151.1 3.3 %copy-start.1 = (bf16[1,256,4096]{2,1,0:T(8,128)(2,1)S(1)}, bf16[1,256,4096]{2,1,0:T(8,128)(2,1)}, u32[]{:S(2)}) copy-start(bf16[1,256,4096]{2,1,0:T(8,128)(2,1)} %get-tuple-element.7) | copy-start | bytes 6291460
  154.4 2.3 %copy-start = (bf16[1,256,4096]{2,1,0:T(8,128)(2,1)S(1)}, bf16[1,256,4096]{2,1,0:T(8,128)(2,1)}, u32[]{:S(2)}) copy-start(bf16[1,256,4096]{2,1,0:T(8,128)(2,1)} %get-tuple-element.8) | copy-start | bytes 6291460

commit v5 on v4

--- a/solution.py
+++ b/solution.py
@@ -1,4 +1,5 @@
 import functools
+import math
 
 import jax
 import jax.numpy as jnp
@@ -38,6 +39,8 @@
     vt_ref,
     s_ref,
     w_ref,
+    ds_ref,
+    scaled_ref,
     dk_ref,
     dv_ref,
     in_send,
@@ -57,7 +60,7 @@
     scale = D_HEAD ** (-0.5)
     nt = (((1,), (1,)), ((), ()))
     nn = (((1,), (0,)), ((), ()))
-    results = (gq_hbm, gk_hbm, gv_hbm)
+    batch = scaled_ref.shape[0] // tok
 
     plane = lax.axis_index("rows")
     share = tok // planes
@@ -172,12 +175,30 @@
         wait_bytes(recv.at[h, 0], in_local.at[h])
         wait_bytes(recv.at[h, pl.ds(0, n - 1), pl.ds(first, 4 - first)], in_recv.at[h])
 
+    def send_query(h, to):
+        cols = columns(me, h)
+
+        @pl.when(to != me)
+        def away():
+            pltpu.make_async_remote_copy(
+                src_ref=outs.at[h, to, 0],
+                dst_ref=gq_hbm.at[0, :, cols],
+                send_sem=out_send,
+                recv_sem=out_recv,
+                device_id={"seq": to},
+                device_id_type=MESH,
+            ).start()
+
+        @pl.when(to == me)
+        def here():
+            pltpu.make_async_copy(outs.at[h, to, 0], gq_hbm.at[0, :, cols], out_local).start()
+
     def send_out(h):
         cols = columns(me, h)
 
         def one(step, carry):
             to = peer(step)
-            for a, dst in enumerate(results):
+            for a, dst in ((1, gk_hbm), (2, gv_hbm)):
                 pltpu.make_async_remote_copy(
                     src_ref=outs.at[h, to, a],
                     dst_ref=dst.at[0, :, cols],
@@ -189,13 +210,14 @@
             return carry
 
         lax.fori_loop(1, n, one, 0)
-        for a, dst in enumerate(results):
+        for a, dst in ((1, gk_hbm), (2, gv_hbm)):
             pltpu.make_async_copy(outs.at[h, me, a], dst.at[0, :, cols], out_local).start()
 
     def attend(h):
         def turn(src, carry):
-            kt_ref[src] = recv[h, src, 1].T
-            vt_ref[src] = recv[h, src, 2].T
+            at = pl.ds(pl.multiple_of(src * tok, tok), tok)
+            kt_ref[:, at] = recv[h, src, 1].T
+            vt_ref[:, at] = recv[h, src, 2].T
             return carry
 
         lax.fori_loop(0, n, turn, 0)
@@ -205,7 +227,9 @@
         picked = lax.broadcasted_iota(jnp.int32, rows.shape, 0) == residue_ref[0]
         added = jnp.sum(jnp.where(picked, rows, 0.0), axis=0, keepdims=True)
 
-        def queries_of(src, carry):
+        def queries_of(group, place):
+            src = group * batch + place
+            cols = pl.ds(pl.multiple_of(place * tok, tok), tok)
             if heads > 2:
 
                 @pl.when((h == 0) & (src == min(3, n - 1)))
@@ -217,46 +241,64 @@
             at = lax.broadcasted_iota(jnp.int32, (tok, D_HEAD), 0) + src * tok
             term = jnp.where(at == pos_ref[0], added, 0.0)
             cot = (recv[h, src, 3].astype(jnp.float32) + term).astype(jnp.bfloat16)
-            top = jnp.full((1, tok), NEG, jnp.float32)
+            top = jnp.full((8, tok), NEG, jnp.float32)
             for c in range(n):
                 scores = lax.dot_general(recv[h, c, 1], q, nt, preferred_element_type=jnp.float32)
                 for b in range(per):
                     part = scores[b * BLOCK : (b + 1) * BLOCK] + bias_ref[src, pl.ds(c * per + b, 1), :]
                     s_ref[c, b * BLOCK : (b + 1) * BLOCK, :] = part
-                    top = jnp.maximum(top, jnp.max(part, axis=0, keepdims=True))
-            total = jnp.zeros((1, tok), jnp.float32)
-            attended = jnp.zeros((D_HEAD, tok), jnp.float32)
+                    top = jnp.maximum(top, jnp.max(part.reshape(BLOCK // 8, 8, tok), axis=0))
+            top = jnp.max(top, axis=0, keepdims=True)
+            total = jnp.zeros((8, tok), jnp.float32)
             for c in range(n):
                 weights = jnp.exp2((s_ref[c] - top) * (scale * LOG2E))
-                total += jnp.sum(weights, axis=0, keepdims=True)
-                weights_bf = weights.astype(jnp.bfloat16)
-                w_ref[c] = weights_bf
-                attended += lax.dot_general(
-                    vt_ref[c], weights_bf, nn, preferred_element_type=jnp.float32
-                )
-            inverse = 1.0 / total
+                total += jnp.sum(weights.reshape(tok // 8, 8, tok), axis=0)
+                w_ref[c, :, cols] = weights.astype(jnp.bfloat16)
+            attended = lax.dot_general(
+                vt_ref[...],
+                w_ref[:, :, cols].reshape(n * tok, tok),
+                nn,
+                preferred_element_type=jnp.float32,
+            )
+            inverse = 1.0 / jnp.sum(total, axis=0, keepdims=True)
             cot_t = (cot.astype(jnp.float32).T * inverse).astype(jnp.bfloat16)
             cot_wide = cot_t.astype(jnp.float32)
-            scaled = cot_wide.T.astype(jnp.bfloat16)
+            scaled_ref[cols, :] = cot_wide.T.astype(jnp.bfloat16)
             delta = inverse * jnp.sum(cot_wide * attended, axis=0, keepdims=True)
-            query_t = jnp.zeros((D_HEAD, tok), jnp.float32)
             for c in range(n):
                 grad_probs = lax.dot_general(
                     recv[h, c, 2], cot_t, nn, preferred_element_type=jnp.float32
                 )
-                weights_bf = w_ref[c]
-                grad_scores = weights_bf * (grad_probs - delta).astype(jnp.bfloat16)
+                ds_ref[c, :, cols] = w_ref[c, :, cols] * (grad_probs - delta).astype(jnp.bfloat16)
+            query_t = lax.dot_general(
+                kt_ref[...],
+                ds_ref[:, :, cols].reshape(n * tok, tok),
+                nn,
+                preferred_element_type=jnp.float32,
+            )
+            outs[h, src, 0] = (scale * query_t.T).astype(jnp.bfloat16)
+            send_query(h, src)
+
+        def batch_of(group, carry):
+            def inner(place, unused):
+                queries_of(group, place)
+                return unused
+
+            lax.fori_loop(0, batch, inner, 0)
+            q_all = recv[h, pl.ds(group * batch, batch), 0].reshape(batch * tok, D_HEAD)
+            cot_all = scaled_ref[...]
+
+            def keys_of(c, unused):
                 dv_ref[c] += lax.dot_general(
-                    weights_bf, scaled, nn, preferred_element_type=jnp.float32
+                    w_ref[c], cot_all, nn, preferred_element_type=jnp.float32
                 )
-                dk_ref[c] += lax.dot_general(grad_scores, q, nn, preferred_element_type=jnp.float32)
-                query_t += lax.dot_general(
-                    kt_ref[c], grad_scores, nn, preferred_element_type=jnp.float32
-                )
-            outs[h, src, 0] = (scale * query_t.T).astype(jnp.bfloat16)
-            return carry
-
-        lax.fori_loop(0, n, queries_of, 0)
+                dk_ref[c] += lax.dot_general(ds_ref[c], q_all, nn, preferred_element_type=jnp.float32)
+                return unused
+
+            lax.fori_loop(0, n, keys_of, 0)
+            return carry
+
+        lax.fori_loop(0, n // batch, batch_of, 0)
 
         def close(src, carry):
             outs[h, src, 1] = (scale * dk_ref[src]).astype(jnp.bfloat16)
@@ -313,6 +355,7 @@
     tok, width = queries.shape
     heads = width // D_HEAD // n
     block_total = tiles.shape[0]
+    batch = math.gcd(4, n)
     hbm = pl.BlockSpec(memory_space=pl.ANY)
     smem = pl.BlockSpec(memory_space=pltpu.SMEM)
     vmem = pl.BlockSpec(memory_space=pltpu.VMEM)
@@ -326,10 +369,12 @@
             pltpu.VMEM((heads, n, 4, tok, D_HEAD), jnp.bfloat16),
             pltpu.VMEM((heads, n, 3, tok, D_HEAD), jnp.bfloat16),
             pltpu.VMEM((n, block_total, tok), jnp.float32),
-            pltpu.VMEM((n, D_HEAD, tok), jnp.bfloat16),
-            pltpu.VMEM((n, D_HEAD, tok), jnp.bfloat16),
+            pltpu.VMEM((D_HEAD, n * tok), jnp.bfloat16),
+            pltpu.VMEM((D_HEAD, n * tok), jnp.bfloat16),
             pltpu.VMEM((n, tok, tok), jnp.float32),
-            pltpu.VMEM((n, tok, tok), jnp.bfloat16),
+            pltpu.VMEM((n, tok, batch * tok), jnp.bfloat16),
+            pltpu.VMEM((n, tok, batch * tok), jnp.bfloat16),
+            pltpu.VMEM((batch * tok, D_HEAD), jnp.bfloat16),
             pltpu.VMEM((n, tok, D_HEAD), jnp.float32),
             pltpu.VMEM((n, tok, D_HEAD), jnp.float32),
             pltpu.SemaphoreType.DMA((heads,)),

time: 161 us -> 166 us (1.031); the launches traced: 158 us -> 165 us
  Pallas kernels: 148 us -> 155 us
    pallas_call x1, Pallas kernels: 148 us -> 155 us  [per_device(): pl.pallas_call(functools.partial(fused_kernel, n, planes, heads), in_spec...]
where the time goes in v5:
time: 166 us; the launch traced here: 165 us
  Pallas kernels  155 us (93%)
  local copies, waits for them, and re-layouts  8.3 us (5%)
  between operations  1.94 us (1%)
    pallas_call x1, Pallas kernels, per_device(): pl.pallas_call(functools.partial(fused_kernel, n, planes, heads), in_spec...  155 us
    unnamed x8, local copies, waits for them, and re-layouts  8.3 us

profile of v5, /device:TPU:0, one launch (start us, length us, event | category | flops | bytes accessed | tf_op | source)
XLA Modules:
  0.0 165.4 jit_solution(11824380069074564081)
XLA Ops:
  1.9 1.4 copy.12.tiles_ref
  3.3 155.2 %fused.1 = (bf16[1,256,4096]{2,1,0:T(8,128)(2,1)}, bf16[1,256,4096]{2,1,0:T(8,128)(2,1)}, bf16[1,256,4096]{2,1,0:T(8,128)(2,1)}) custom-call(s32[1]{0:T(128)S(6)} %copy.16.pos_ref, s32[1]{0:T(128)S(6)} %copy.17.residue_ref, s32[16,8]{1,0:T(8,128)} %copy.12.tiles_ref, s32[16]{0:T(128)} %counts_ref.1, bf16[33,4096]{1,0:T(8,128)(2,1)} %table_ref.1, ...), custom_call_target="tpu_custom_call" | custom-call | tf_op jit(solution)/shard_map/fused/pallas_call | solution.py:363
  158.4 0.0 copy-start.1
  158.5 3.3 %copy.18 = bf16[1,256,4096]{2,1,0:T(8,128)(2,1)} copy(bf16[1,256,4096]{2,1,0:T(8,128)(2,1)} %get-tuple-element.6) | data formatting | bytes 4194304
  161.7 0.0 copy-done.1
  161.7 0.0 copy-start
  161.7 1.3 copy.19
  163.1 1.0 copy-done
  164.1 1.3 copy.20
Async XLA Ops:
  158.4 3.3 %copy-start.1 = (bf16[1,256,4096]{2,1,0:T(8,128)(2,1)S(1)}, bf16[1,256,4096]{2,1,0:T(8,128)(2,1)}, u32[]{:S(2)}) copy-start(bf16[1,256,4096]{2,1,0:T(8,128)(2,1)} %get-tuple-element.7) | copy-start | bytes 6291460
  161.7 2.3 %copy-start = (bf16[1,256,4096]{2,1,0:T(8,128)(2,1)S(1)}, bf16[1,256,4096]{2,1,0:T(8,128)(2,1)}, u32[]{:S(2)}) copy-start(bf16[1,256,4096]{2,1,0:T(8,128)(2,1)} %get-tuple-element.8) | copy-start | bytes 6291460

commit v6 on v5

--- a/solution.py
+++ b/solution.py
@@ -41,6 +41,7 @@
     w_ref,
     ds_ref,
     scaled_ref,
+    q_ref,
     dk_ref,
     dv_ref,
     in_send,
@@ -228,16 +229,18 @@
         added = jnp.sum(jnp.where(picked, rows, 0.0), axis=0, keepdims=True)
 
         def queries_of(group, place):
-            src = group * batch + place
+            spot = group * batch + place
+            src = lax.rem(me + spot, n)
             cols = pl.ds(pl.multiple_of(place * tok, tok), tok)
             if heads > 2:
 
-                @pl.when((h == 0) & (src == min(3, n - 1)))
+                @pl.when((h == 0) & (spot == min(3, n - 1)))
                 def onward():
                     for later in range(2, heads):
                         forward(later)
 
             q = recv[h, src, 0]
+            q_ref[cols, :] = q
             at = lax.broadcasted_iota(jnp.int32, (tok, D_HEAD), 0) + src * tok
             term = jnp.where(at == pos_ref[0], added, 0.0)
             cot = (recv[h, src, 3].astype(jnp.float32) + term).astype(jnp.bfloat16)
@@ -285,7 +288,7 @@
                 return unused
 
             lax.fori_loop(0, batch, inner, 0)
-            q_all = recv[h, pl.ds(group * batch, batch), 0].reshape(batch * tok, D_HEAD)
+            q_all = q_ref[...]
             cot_all = scaled_ref[...]
 
             def keys_of(c, unused):
@@ -350,6 +353,15 @@
     wait_bytes(outs.at[:, 0], out_local)
 
 
+def hand_on(a_ref, b_ref, c_ref, a_out, b_out, c_out, sems):
+    pairs = ((a_ref, a_out), (b_ref, b_out), (c_ref, c_out))
+    copies = [pltpu.make_async_copy(src, dst, sems.at[i]) for i, (src, dst) in enumerate(pairs)]
+    for copy in copies:
+        copy.start()
+    for copy in copies:
+        copy.wait()
+
+
 def per_device(queries, keys, values, grad_out, table, positions, residues, tiles, counts):
     n, planes = lax.axis_size("seq"), lax.axis_size("rows")
     tok, width = queries.shape
@@ -360,7 +372,7 @@
     smem = pl.BlockSpec(memory_space=pltpu.SMEM)
     vmem = pl.BlockSpec(memory_space=pltpu.VMEM)
     shape = jax.ShapeDtypeStruct((1, tok, width), jnp.bfloat16)
-    return pl.pallas_call(
+    results = pl.pallas_call(
         functools.partial(fused_kernel, n, planes, heads),
         in_specs=[smem, smem, smem, smem, vmem, hbm, hbm, hbm, hbm],
         out_specs=[hbm] * 3,
@@ -375,6 +387,7 @@
             pltpu.VMEM((n, tok, batch * tok), jnp.bfloat16),
             pltpu.VMEM((n, tok, batch * tok), jnp.bfloat16),
             pltpu.VMEM((batch * tok, D_HEAD), jnp.bfloat16),
+            pltpu.VMEM((batch * tok, D_HEAD), jnp.bfloat16),
             pltpu.VMEM((n, tok, D_HEAD), jnp.float32),
             pltpu.VMEM((n, tok, D_HEAD), jnp.float32),
             pltpu.SemaphoreType.DMA((heads,)),
@@ -393,6 +406,14 @@
         ),
         name="fused",
     )(positions, residues, tiles, counts, table, queries, keys, values, grad_out)
+    return pl.pallas_call(
+        hand_on,
+        in_specs=[hbm] * 3,
+        out_specs=[hbm] * 3,
+        out_shape=[shape] * 3,
+        scratch_shapes=[pltpu.SemaphoreType.DMA((3,))],
+        name="hand_on",
+    )(*results)
 
 
 def solution(mesh):

time: 166 us -> 350 us (2.11)
  Pallas kernels: 155 us -> 347 us
  local copies, waits for them, and re-layouts: 8.3 us -> 1.36 us
    pallas_call x0 -> x1, Pallas kernels: none -> 192 us  [per_device(): pl.pallas_call(hand_on, in_specs=[hbm] * 3, out_specs=[hbm] * 3, out_shap...]
    unnamed x8 -> x1, local copies, waits for them, and re-layouts: 8.3 us -> 1.36 us
where the time goes in v6:
time: 350 us
  Pallas kernels  347 us (99%)
    pallas_call x1, Pallas kernels, per_device(): pl.pallas_call(hand_on, in_specs=[hbm] * 3, out_specs=[hbm] * 3, out_shap...  192 us
    pallas_call x1, Pallas kernels, per_device(): pl.pallas_call(functools.partial(fused_kernel, n, planes, heads), in_spec...  155 us

profile of v6, /device:TPU:0, one launch (start us, length us, event | category | flops | bytes accessed | tf_op | source)
XLA Modules:
  0.0 350.2 jit_solution(17535880119566416079)
XLA Ops:
  1.9 1.4 copy.12.tiles_ref
  3.3 155.2 %fused.1 = (bf16[1,256,4096]{2,1,0:T(8,128)(2,1)}, bf16[1,256,4096]{2,1,0:T(8,128)(2,1)}, bf16[1,256,4096]{2,1,0:T(8,128)(2,1)}) custom-call(s32[1]{0:T(128)S(6)} %copy.13.pos_ref, s32[1]{0:T(128)S(6)} %copy.14.residue_ref, s32[16,8]{1,0:T(8,128)} %copy.12.tiles_ref, s32[16]{0:T(128)} %counts_ref.1, bf16[33,4096]{1,0:T(8,128)(2,1)} %table_ref.1, ...), custom_call_target="tpu_custom_call" | custom-call | tf_op jit(solution)/shard_map/fused/pallas_call | solution.py:375
  158.5 191.7 %hand_on.1 = (bf16[1,256,4096]{2,1,0:T(8,128)(2,1)}, bf16[1,256,4096]{2,1,0:T(8,128)(2,1)}, bf16[1,256,4096]{2,1,0:T(8,128)(2,1)}) custom-call(bf16[1,256,4096]{2,1,0:T(8,128)(2,1)} %get-tuple-element.6.a_ref, bf16[1,256,4096]{2,1,0:T(8,128)(2,1)} %get-tuple-element.7.b_ref, bf16[1,256,4096]{2,1,0:T(8,128)(2,1)} %get-tuple-element.8.c_ref), custom_call_target="tpu_custom_call" | custom-call | tf_op jit(solution)/shard_map/hand_on/pallas_call | solution.py:409

commit v7 on v4

--- a/solution.py
+++ b/solution.py
@@ -57,7 +57,6 @@
     scale = D_HEAD ** (-0.5)
     nt = (((1,), (1,)), ((), ()))
     nn = (((1,), (0,)), ((), ()))
-    results = (gq_hbm, gk_hbm, gv_hbm)
 
     plane = lax.axis_index("rows")
     share = tok // planes
@@ -172,12 +171,30 @@
         wait_bytes(recv.at[h, 0], in_local.at[h])
         wait_bytes(recv.at[h, pl.ds(0, n - 1), pl.ds(first, 4 - first)], in_recv.at[h])
 
+    def send_query(h, to):
+        cols = columns(me, h)
+
+        @pl.when(to != me)
+        def away():
+            pltpu.make_async_remote_copy(
+                src_ref=outs.at[h, to, 0],
+                dst_ref=gq_hbm.at[0, :, cols],
+                send_sem=out_send,
+                recv_sem=out_recv,
+                device_id={"seq": to},
+                device_id_type=MESH,
+            ).start()
+
+        @pl.when(to == me)
+        def here():
+            pltpu.make_async_copy(outs.at[h, to, 0], gq_hbm.at[0, :, cols], out_local).start()
+
     def send_out(h):
         cols = columns(me, h)
 
         def one(step, carry):
             to = peer(step)
-            for a, dst in enumerate(results):
+            for a, dst in ((1, gk_hbm), (2, gv_hbm)):
                 pltpu.make_async_remote_copy(
                     src_ref=outs.at[h, to, a],
                     dst_ref=dst.at[0, :, cols],
@@ -189,7 +206,7 @@
             return carry
 
         lax.fori_loop(1, n, one, 0)
-        for a, dst in enumerate(results):
+        for a, dst in ((1, gk_hbm), (2, gv_hbm)):
             pltpu.make_async_copy(outs.at[h, me, a], dst.at[0, :, cols], out_local).start()
 
     def attend(h):
@@ -205,10 +222,11 @@
         picked = lax.broadcasted_iota(jnp.int32, rows.shape, 0) == residue_ref[0]
         added = jnp.sum(jnp.where(picked, rows, 0.0), axis=0, keepdims=True)
 
-        def queries_of(src, carry):
+        def queries_of(spot, carry):
+            src = lax.rem(me + spot, n)
             if heads > 2:
 
-                @pl.when((h == 0) & (src == min(3, n - 1)))
+                @pl.when((h == 0) & (spot == min(3, n - 1)))
                 def onward():
                     for later in range(2, heads):
                         forward(later)
@@ -254,6 +272,7 @@
                     kt_ref[c], grad_scores, nn, preferred_element_type=jnp.float32
                 )
             outs[h, src, 0] = (scale * query_t.T).astype(jnp.bfloat16)
+            send_query(h, src)
             return carry
 
         lax.fori_loop(0, n, queries_of, 0)

time: 161 us -> 157 us (0.975)
  Pallas kernels: 148 us -> 145 us
    pallas_call x1, Pallas kernels: 148 us -> 145 us  [per_device(): pl.pallas_call(functools.partial(fused_kernel, n, planes, heads), in_spec...]
where the time goes in v7:
time: 157 us; the launch traced here: 155 us
  Pallas kernels  145 us (92%)
  local copies, waits for them, and re-layouts  8.3 us (5%)
  between operations  1.94 us (1%)
    pallas_call x1, Pallas kernels, per_device(): pl.pallas_call(functools.partial(fused_kernel, n, planes, heads), in_spec...  145 us
    unnamed x8, local copies, waits for them, and re-layouts  8.3 us

profile of v7, /device:TPU:0, one launch (start us, length us, event | category | flops | bytes accessed | tf_op | source)
XLA Modules:
  0.0 154.9 jit_solution(7551243230948126655)
XLA Ops:
  1.9 1.4 copy.12.tiles_ref
  3.3 144.7 %fused.1 = (bf16[1,256,4096]{2,1,0:T(8,128)(2,1)}, bf16[1,256,4096]{2,1,0:T(8,128)(2,1)}, bf16[1,256,4096]{2,1,0:T(8,128)(2,1)}) custom-call(s32[1]{0:T(128)S(6)} %copy.16.pos_ref, s32[1]{0:T(128)S(6)} %copy.17.residue_ref, s32[16,8]{1,0:T(8,128)} %copy.12.tiles_ref, s32[16]{0:T(128)} %counts_ref.1, bf16[33,4096]{1,0:T(8,128)(2,1)} %table_ref.1, ...), custom_call_target="tpu_custom_call" | custom-call | tf_op jit(solution)/shard_map/fused/pallas_call | solution.py:339
  147.9 0.0 copy-start.1
  147.9 3.3 %copy.18 = bf16[1,256,4096]{2,1,0:T(8,128)(2,1)} copy(bf16[1,256,4096]{2,1,0:T(8,128)(2,1)} %get-tuple-element.6) | data formatting | bytes 4194304
  151.2 0.0 copy-done.1
  151.2 0.0 copy-start
  151.2 1.3 copy.19
  152.5 1.0 copy-done
  153.6 1.3 copy.20
Async XLA Ops:
  147.9 3.3 %copy-start.1 = (bf16[1,256,4096]{2,1,0:T(8,128)(2,1)S(1)}, bf16[1,256,4096]{2,1,0:T(8,128)(2,1)}, u32[]{:S(2)}) copy-start(bf16[1,256,4096]{2,1,0:T(8,128)(2,1)} %get-tuple-element.7) | copy-start | bytes 6291460
  151.2 2.3 %copy-start = (bf16[1,256,4096]{2,1,0:T(8,128)(2,1)S(1)}, bf16[1,256,4096]{2,1,0:T(8,128)(2,1)}, u32[]{:S(2)}) copy-start(bf16[1,256,4096]{2,1,0:T(8,128)(2,1)} %get-tuple-element.8) | copy-start | bytes 6291460
